TPU v7x, 256 devices: a whole 4x4x8 slice. The times are simulated.
256 devices in a mesh: dp: 2 (over z_lo), seq: 128 (over x, z_hi, y, core).
Axes of the slice: x: 4, y: 4, z: 8 (z_hi: 4, z_lo: 2; z = z_hi * 2 + z_lo), core: 2. Of those that a mesh axis runs over, the one named last changes fastest.
Arguments:
- inputs: bfloat16 [2, 131072, 1024], P('dp', 'seq'), may hold values from -24 to 24
- cotangent: bfloat16 [2, 131072, 1024], P('dp', 'seq'), may hold values from -0.29882812 to 0.29882812
- w_value: bfloat16 [1024, 1024], P('seq'), may hold values from -0.1875 to 0.1875
- right_factor: bfloat16 [256, 512, 512], P('seq'), may hold values from -0.25 to 0.25
- left_factor: bfloat16 [512, 256, 256], P('seq'), may hold values from -0.375 to 0.375
Outputs:
- mixed: bfloat16 [2, 131072, 1024], P('dp', 'seq')
- input_grad: bfloat16 [2, 131072, 1024], P('dp', 'seq')
- right_grad: float32 [256, 512, 512], P('seq')
- left_grad: float32 [512, 256, 256], P('seq')
- weight_grad: float32 [1024, 1024], P('seq')
All inputs are finite; a program needn't handle non-finite values.
Results may differ from a plain program's by a relative error of at most 0.0064.
Values may be sent and summed in bfloat16 or wider, within the bound.
A program may use at most 128 MiB of HBM per device.

v0:
```python
import jax
import jax.numpy as jnp
from jax import lax
from jax.sharding import PartitionSpec as P


def to_blocks(array):
    return lax.all_to_all(array, "seq", split_axis=2, concat_axis=1, tiled=True)


def to_rows(array):
    return lax.all_to_all(array, "seq", split_axis=1, concat_axis=2, tiled=True)


def body(inputs, cotangent, w_value, right_factor, left_factor):
    seq_count, tok_count, width = inputs.shape
    outer_local = right_factor.shape[0]
    inner_size = right_factor.shape[1]
    tok_rows = inputs.reshape(seq_count * tok_count, width)
    whole_weight = lax.all_gather(w_value, "seq", axis=0, tiled=True)
    value = jnp.dot(tok_rows, whole_weight, preferred_element_type=jnp.float32).astype(jnp.bfloat16)
    value_grid = value.reshape(seq_count, outer_local, inner_size, width)
    first = jnp.einsum(
        "abc,sacd->sabd", right_factor, value_grid, preferred_element_type=jnp.float32
    ).astype(jnp.bfloat16)
    first_cols = to_blocks(first)
    second_cols = jnp.einsum(
        "bxy,sybd->sxbd", left_factor, first_cols, preferred_element_type=jnp.float32
    ).astype(jnp.bfloat16)
    second = to_rows(second_cols).reshape(seq_count, tok_count, width)
    inputs32 = inputs.astype(jnp.float32)
    upstream32 = cotangent.astype(jnp.float32)
    mixed = (inputs32 * second.astype(jnp.float32)).astype(jnp.bfloat16)
    second_grad = (upstream32 * inputs32).astype(jnp.bfloat16)
    grad_cols = to_blocks(second_grad.reshape(seq_count, outer_local, inner_size, width))
    first_grad_cols = jnp.einsum(
        "bxy,sxbd->sybd", left_factor, grad_cols, preferred_element_type=jnp.float32
    ).astype(jnp.bfloat16)
    left_grad = jnp.einsum(
        "sxbd,sybd->bxy", grad_cols, first_cols, preferred_element_type=jnp.float32
    )
    first_grad = to_rows(first_grad_cols)
    value_grad = jnp.einsum(
        "abc,sabd->sacd", right_factor, first_grad, preferred_element_type=jnp.float32
    ).astype(jnp.bfloat16)
    right_grad = jnp.einsum(
        "sabd,sacd->abc", first_grad, value_grid, preferred_element_type=jnp.float32
    )
    grad_rows_flat = value_grad.reshape(seq_count * tok_count, width)
    back = lax.dot_general(
        grad_rows_flat, whole_weight, (((1,), (1,)), ((), ())), preferred_element_type=jnp.float32
    )
    back = back.reshape(seq_count, tok_count, width)
    input_grad = (upstream32 * second.astype(jnp.float32) + back).astype(jnp.bfloat16)
    whole_grad = lax.dot_general(
        tok_rows, grad_rows_flat, (((0,), (0,)), ((), ())), preferred_element_type=jnp.float32
    )
    right_grad, left_grad, whole_grad = lax.psum((right_grad, left_grad, whole_grad), "dp")
    weight_grad = lax.psum_scatter(whole_grad, "seq", scatter_dimension=0, tiled=True)
    return (mixed, input_grad, right_grad, left_grad, weight_grad)


def solution(mesh):
    placed = (
        P("dp", "seq", None),
        P("dp", "seq", None),
        P("seq", None),
        P("seq", None, None),
        P("seq", None, None),
    )
    return jax.shard_map(
        body,
        mesh=mesh,
        in_specs=placed,
        out_specs=(
            P("dp", "seq", None),
            P("dp", "seq", None),
            P("seq", None, None),
            P("seq", None, None),
            P("seq", None),
        ),
        check_vma=False,
    )
```

profile of v0, /device:TPU:1, one launch (start us, length us, event | category | flops | bytes accessed | tf_op | source)
XLA Modules:
  0.0 1207.8 jit_solution(7047450017384815217)
XLA Ops:
  8.0 84.5 %all-gather.2.cloned.1.call-done = bf16[1024,1024]{1,0:T(8,128)(2,1)} async-done(((bf16[8,1024]{1,0:T(8,128)(2,1)}), bf16[1024,1024]{1,0:T(8,128)(2,1)}) %all-gather.2.cloned.1.call-update) | async-done | bytes 2097168 | tf_op jit(solution)/shard_map/all_gather | solution.py:20
  92.5 4.5 fusion.7
  97.1 1.3 copy-done.9
  98.3 2.9 convert_bitcast_fusion.3
  101.3 5.0 copy.34
  106.3 60.5 %all_to_all.54 = bf16[1,2,512,1024]{3,1,0,2:T(2,128)(2,1)S(1)} all-to-all(bf16[1,2,512,1024]{3,1,0,2:T(2,128)(2,1)S(1)} %copy.34), channel_id=1, replica_groups=mesh['dp'=2,'seq'=128] {'seq'}, dimensions={2} | all-to-all | bytes 4194304 | tf_op jit(solution)/shard_map/all_to_all | solution.py:8
  168.0 2.8 convert_bitcast_fusion.2
  170.8 4.5 copy.37
  175.3 52.3 %all_to_all.55 = bf16[1,256,4,1024]{3,2,0,1:T(4,128)(2,1)S(1)} all-to-all(bf16[1,256,4,1024]{3,2,0,1:T(4,128)(2,1)} %copy.37), channel_id=1, replica_groups=mesh['dp'=2,'seq'=128] {'seq'}, dimensions={1} | all-to-all | bytes 4194304 | tf_op jit(solution)/shard_map/all_to_all | solution.py:12
  228.7 2.9 copy.38
  231.6 5.3 reshape.81
  236.9 6.2 fusion.3
  243.0 2.2 copy.39
  245.2 59.5 %all_to_all.56 = bf16[1,2,512,1024]{3,1,0,2:T(2,128)(2,1)S(1)} all-to-all(bf16[1,2,512,1024]{3,1,0,2:T(2,128)(2,1)S(1)} %copy.39), channel_id=1, replica_groups=mesh['dp'=2,'seq'=128] {'seq'}, dimensions={2} | all-to-all | bytes 4194304 | tf_op jit(solution)/shard_map/all_to_all | solution.py:8
  305.9 1.3 copy-done.2
  307.2 2.8 convert_bitcast_fusion.1
  310.0 4.5 copy.42
  314.5 59.7 %all_to_all.57 = bf16[1,256,4,1024]{3,2,0,1:T(4,128)(2,1)S(1)} all-to-all(bf16[1,256,4,1024]{3,2,0,1:T(4,128)(2,1)} %copy.42), channel_id=1, replica_groups=mesh['dp'=2,'seq'=128] {'seq'}, dimensions={1} | all-to-all | bytes 4194304 | tf_op jit(solution)/shard_map/all_to_all | solution.py:12
  374.2 2.0 copy.43
  376.3 3.9 reshape.78
  380.2 3.0 convolution_convert_fusion
  383.3 1.3 copy-done.11
  384.6 4.3 convolution_bitcast_fusion
  388.9 5.4 copy.50
  394.4 4.0 fusion.11
  398.4 2.6 fusion.15
  401.0 1.6 copy-done.7
  402.6 7.2 fusion.2
  409.7 686.3 %reduce-scatter.4.cloned.1.call-done = f32[8,1024]{1,0:T(8,128)} async-done(((f32[1024,1024]{1,0:T(8,128)}), f32[8,1024]{1,0:T(8,128)}) %reduce-scatter.4.cloned.1.call-update) | async-done | bytes 32784
  1097.0 12.0 psum.24
  1109.8 87.2 %all-reduce.3.cloned.1.call-done = (f32[2,512,512]{2,1,0:T(8,128)}, f32[4,256,256]{2,1,0:T(8,128)}) async-done(((f32[2,512,512]{2,1,0:T(8,128)}, f32[4,256,256]{2,1,0:T(8,128)}), (f32[2,512,512]{2,1,0:T(8,128)}, f32[4,256,256]{2,1,0:T(8,128)})) %all-reduce.3.cloned.1.call-update) | async-done | bytes 3145744 | tf_op jit(solution)/shard_map/psum | solution.py:58
  1197.0 3.2 copy.62
  (32 shorter events, 7.0 us)
Async XLA Ops:
  7.2 91.2 %copy-start = (bf16[2,512,512]{2,1,0:T(8,128)(2,1)S(1)}, bf16[2,512,512]{2,1,0:T(8,128)(2,1)}, u32[]{:S(2)}) copy-start(bf16[2,512,512]{2,1,0:T(8,128)(2,1)} %param.8) | copy-start | bytes 3145732
  7.2 85.3 %all-gather.2.cloned.1.call-start = ((), (), s32[]{:S(2)}) async-start(), calls=%async_computation.5 | async-start | bytes 2113536 | tf_op jit(solution)/shard_map/all_gather | solution.py:20
  7.9 1088.1 %reduce-scatter.4.cloned.1.call-start = ((), (), s32[]{:S(2)}) async-start(), calls=%async_computation.6 | async-start | bytes 4227072
  97.0 1.3 copy-start.9
  166.8 1.2 copy-start.3
  304.7 2.5 copy-start.4
  305.9 1.3 copy-start.2
  380.2 4.4 copy-start.6
  383.2 1.3 copy-start.11
  394.3 802.7 %all-reduce.3.cloned.1.call-start = ((), (), s32[]{:S(2)}) async-start(), calls=%async_computation.7 | async-start | bytes 6291456 | tf_op jit(solution)/shard_map/psum | solution.py:58
  394.4 4.0 copy-start.5
  394.4 4.0 copy-start.10
  401.0 1.6 copy-start.7
  1197.0 3.2 copy-start.8
  1197.0 4.2 copy-start.1
Sparse Core Ops, SparseCore 0:
  11.6 80.8 all-gather.1
  394.4 701.5 reduce-scatter.3
  1099.5 97.5 all-reduce.2
where the time goes:
time: 1210 us
  waiting for transfers between devices  859 us (71%)
  blocking collectives  244 us (20%)
  local copies, waits for them, and re-layouts  49.6 us (4%)
  matrix products  34.1 us (3%)
  between operations  13.9 us (1%)
    unnamed x4, waiting for transfers between devices  687 us
    all_to_all x2, blocking collectives, to_blocks(): return lax.all_to_all(array, 'seq', split_axis=2, concat_axis=1, tiled=True)  120 us
    all_to_all x2, blocking collectives, to_rows(): return lax.all_to_all(array, 'seq', split_axis=1, concat_axis=2, tiled=True)  112 us
    psum x1, waiting for transfers between devices, body(): lax.psum((right_grad, left_grad, whole_grad), 'dp')  87.2 us
    all_gather x1, waiting for transfers between devices, body(): whole_weight = lax.all_gather(w_value, 'seq', axis=0, tiled=True)  84.5 us
  transfers between devices with their start and end apart: 3, of which 3 were waited for; matrix products, arithmetic and copies ran while one was open for 1% of the time, Pallas kernels for 0%

commit v1 on v0

v1 whole, which is shorter than its diff:
```python
import jax
import jax.numpy as jnp
from jax import lax
from jax.experimental import pallas as pl
from jax.experimental.pallas import tpu as pltpu
from jax.sharding import PartitionSpec as P

MESH = pl.DeviceIdType.MESH
F32 = jnp.float32
BF16 = jnp.bfloat16
N = 128
X4, Z4, Y4, C2 = 4, 4, 4, 2


def seq_of(x, z, y, c):
    return ((x * Z4 + z) * Y4 + y) * C2 + c


def dot(a, b, ca=1, cb=0):
    return lax.dot_general(a, b, (((ca,), (cb,)), ((), ())), preferred_element_type=F32)


def pack(x):
    return jnp.concatenate([x[:, :, :256], x[:, :, 256:]], axis=1).astype(BF16)


def unpack(w):
    w = w.astype(F32)
    return jnp.concatenate([w[:, :8, :], w[:, 8:, :]], axis=2)


def low_rows(shape):
    return lax.broadcasted_iota(jnp.int32, shape, 1) < 4


def interleave(t0, t1):
    low = low_rows(t0.shape)
    even = jnp.where(low, t0, pltpu.roll(t1, 4, 1))
    odd = jnp.where(low, pltpu.roll(t0, 4, 1), t1)
    return jnp.stack([even, odd], axis=1).reshape(2 * t0.shape[0], 8, t0.shape[2])


def deinterleave(w):
    pair = w.reshape(w.shape[0] // 2, 2, 8, w.shape[2])
    even, odd = pair[:, 0], pair[:, 1]
    low = low_rows(even.shape)
    return jnp.where(low, even, pltpu.roll(odd, 4, 1)), jnp.where(low, pltpu.roll(even, 4, 1), odd)


def loop(count, step):
    def run(i, carry):
        step(i)
        return carry

    lax.fori_loop(0, count, run, 0)


def at(i, size):
    return pl.ds(pl.multiple_of(i * size, size), size)


def mixer(
    x_ref, u_ref, w_ref, r_ref, l_ref,
    mixed_hbm, igrad_hbm, rgrad_hbm, lgrad_hbm, wgrad_ref,
    s1, r1, s2, r2, s3, r3, s4, r4,
    wall, wm, m_ref, mt_ref, t_ref, g_ref, f_ref, v_ref, fg_ref, vg_ref,
    lg_big, lg_mid, lg_own, lg_other, lg_sum, rg_own, rg_other, rg_sum,
    core_in, plane_out, plane_in, z_out, z_in, back_ref, mixed_ref, igrad_ref,
    send_sem, recv_sem, own_sem, w_sem, x_sem, out_sem,
):
    me = lax.axis_index("seq")
    dp = lax.axis_index("dp")
    x = lax.div(me, 32)
    z = lax.rem(lax.div(me, 8), 4)
    y = lax.rem(lax.div(me, 2), 4)
    c = lax.rem(me, 2)

    def remote(src, dst, send, recv, target, group=None):
        return pltpu.make_async_remote_copy(
            src_ref=src, dst_ref=dst, send_sem=send, recv_sem=recv,
            device_id=(dp if group is None else group, target), device_id_type=MESH,
        )

    def settle(ref, sem):
        pltpu.make_async_copy(ref, ref, sem).wait()

    def exchange(i, src, dst):
        pltpu.make_async_copy(src.at[me], dst.at[me], own_sem.at[i]).start()

        def send(k):
            d = lax.rem(me + k + 1, N)
            remote(src.at[d], dst.at[me], send_sem.at[i], recv_sem.at[i], d).start()

        loop(N - 1, send)

    def arrived(i, src, dst):
        pltpu.make_async_copy(src.at[me], dst.at[me], own_sem.at[i]).wait()
        settle(dst.at[pl.ds(0, N - 1)], recv_sem.at[i])

    def sent(i, src):
        settle(src.at[pl.ds(0, N - 1)], send_sem.at[i])

    for m in range(2):
        rows = w_ref[:, 512 * m : 512 * m + 512].astype(F32).reshape(1, 8, 512)
        wall[x, z, y, c, :, 256 * m : 256 * m + 256] = pack(rows).reshape(16, 256)

    def spread(phase, block, targets):
        for t in targets:
            remote(block, block, w_sem.at[2 * phase], w_sem.at[2 * phase + 1], t).start()

    def spread_done(phase, like):
        settle(like, w_sem.at[2 * phase + 1])
        settle(like, w_sem.at[2 * phase])

    spread(0, wall.at[x, z, y, c], [seq_of(x, lax.rem(z + i, 4), y, c) for i in (1, 2, 3)])

    def second_grad(i):
        a0, a1 = at(i, 32), pl.ds(pl.multiple_of(512 + i * 32, 32), 32)
        for m in range(2):
            cols = slice(512 * m, 512 * m + 512)
            t0 = x_ref[a0, cols].astype(F32) * u_ref[a0, cols].astype(F32)
            t1 = x_ref[a1, cols].astype(F32) * u_ref[a1, cols].astype(F32)
            both = interleave(t0.reshape(4, 8, 512), t1.reshape(4, 8, 512))
            s1[at(i, 8), :, 256 * m : 256 * m + 256] = pack(both)

    loop(16, second_grad)
    exchange(0, s1, r1)

    def widen(b):
        select = (
            lax.broadcasted_iota(jnp.int32, (256, 1024), 1)
            == 4 * lax.broadcasted_iota(jnp.int32, (256, 1024), 0) + b
        ).astype(F32).astype(BF16)
        return select

    def place(i):
        row = lax.broadcasted_iota(jnp.int32, (256, 1024), 0) + i * 256
        col = lax.broadcasted_iota(jnp.int32, (256, 1024), 1)
        return (4 * lax.rem(col, 256) + lax.div(col, 256) == row).astype(F32).astype(BF16)

    def build(transposed, out):
        def wide(b):
            t_ref[at(b, 256), :] = dot(l_ref[b], widen(b), ca=0 if transposed else 1).astype(BF16)

        loop(4, wide)

        def rows(i):
            out[at(i, 256), :] = dot(place(i), t_ref[...]).astype(BF16)

        loop(4, rows)

    spread_done(0, wall.at[0, pl.ds(0, 3), 0, 0])
    spread(1, wall.at[x, :, y, c], [seq_of(lax.rem(x + i, 4), z, y, c) for i in (1, 2, 3)])
    build(True, mt_ref)
    spread_done(1, wall.at[pl.ds(0, 3), :, 0, 0])
    spread(2, wall.at[:, :, y, c], [seq_of(x, z, lax.rem(y + i, 4), c) for i in (1, 2, 3)])
    build(False, m_ref)
    spread_done(2, wall.at[:, :, pl.ds(0, 3), 0])
    spread(3, wall.at[:, :, :, c], [seq_of(x, z, y, 1 - c)])
    spread_done(3, wall.at[:, :, :, 0])

    def unpack_weight(i):
        for m in range(2):
            part = wall[i, :, :, :, :, 256 * m : 256 * m + 256].reshape(32, 16, 256)
            wm[at(i, 256), 512 * m : 512 * m + 512] = unpack(part).reshape(256, 512).astype(BF16)

    loop(4, unpack_weight)

    def value(i):
        v_ref[at(i, 256), :] = dot(x_ref[at(i, 256), :], wm[...]).astype(BF16)

    loop(4, value)

    def first(i):
        for m in range(2):
            cols = slice(512 * m, 512 * m + 512)
            t0 = dot(r_ref[0, at(i, 256), :], v_ref[0:512, cols])
            t1 = dot(r_ref[1, at(i, 256), :], v_ref[512:1024, cols])
            both = interleave(t0.reshape(32, 8, 512), t1.reshape(32, 8, 512))
            s2[at(i, 64), :, 256 * m : 256 * m + 256] = pack(both)

    loop(2, first)
    exchange(1, s2, r2)

    def unpack_all(src, dst):
        def step(i):
            for m in range(2):
                part = src[at(i, 16), :, 256 * m : 256 * m + 256]
                dst[at(i, 128), 512 * m : 512 * m + 512] = unpack(part).reshape(128, 512).astype(BF16)

        loop(8, step)

    def columns_product(big, cols_ref, out):
        def step(i):
            for m in range(2):
                t = dot(big[at(i, 256), :], cols_ref[:, 512 * m : 512 * m + 512])
                out[at(i, 32), :, 256 * m : 256 * m + 256] = pack(t.reshape(32, 8, 512))

        loop(4, step)

    arrived(0, s1, r1)
    unpack_all(r1, g_ref)
    columns_product(mt_ref, g_ref, s3)
    exchange(2, s3, r3)

    arrived(1, s2, r2)
    unpack_all(r2, f_ref)
    columns_product(m_ref, f_ref, s4)
    exchange(3, s4, r4)

    def left_all(i):
        rows = dot(g_ref[at(i, 256), :], f_ref[...], cb=1)
        row = lax.broadcasted_iota(jnp.int32, (256, 1024), 0)
        col = lax.broadcasted_iota(jnp.int32, (256, 1024), 1)
        lg_big[at(i, 256), :] = jnp.where(lax.rem(row, 4) == lax.rem(col, 4), rows, 0.0).astype(BF16)

    loop(4, left_all)

    def left_narrow(i):
        c_row = lax.broadcasted_iota(jnp.int32, (1024, 256), 0)
        c_col = lax.broadcasted_iota(jnp.int32, (1024, 256), 1)
        narrow = (lax.div(c_row, 4) == c_col).astype(F32).astype(BF16)
        lg_mid[at(i, 256), :] = dot(lg_big[at(i, 256), :], narrow).astype(BF16)

    loop(4, left_narrow)

    def left_place(b):
        row = lax.broadcasted_iota(jnp.int32, (256, 1024), 0)
        col = lax.broadcasted_iota(jnp.int32, (256, 1024), 1)
        take = (4 * row + b == col).astype(F32).astype(BF16)
        lg_own[b] = dot(take, lg_mid[...]).astype(BF16)

    loop(4, left_place)
    left_swap = remote(lg_own, lg_other, x_sem.at[0], x_sem.at[1], me, 1 - dp)
    left_swap.start()

    arrived(2, s3, r3)

    def first_grad(i):
        for m in range(2):
            t0, t1 = deinterleave(unpack(r3[at(i, 16), :, 256 * m : 256 * m + 256]))
            cols = slice(512 * m, 512 * m + 512)
            fg_ref[at(i, 64), cols] = t0.reshape(64, 512).astype(BF16)
            fg_ref[pl.ds(pl.multiple_of(512 + i * 64, 64), 64), cols] = t1.reshape(64, 512).astype(BF16)

    loop(8, first_grad)

    def right_part(i):
        rg_own[i] = dot(fg_ref[at(i, 512), :], v_ref[at(i, 512), :], cb=1).astype(BF16)

    loop(2, right_part)
    right_swap = remote(rg_own, rg_other, x_sem.at[2], x_sem.at[3], me, 1 - dp)
    right_swap.start()

    def value_grad(i):
        vg_ref[at(i, 512), :] = dot(r_ref[i], fg_ref[at(i, 512), :], ca=0).astype(BF16)

    loop(2, value_grad)

    def weight_part(i):
        for m in range(2):
            t = dot(x_ref[:, at(i, 256)], vg_ref[:, 512 * m : 512 * m + 512], ca=0)
            wall[i, :, :, :, :, 256 * m : 256 * m + 256] = pack(t.reshape(32, 8, 512)).reshape(4, 4, 2, 16, 256)

    loop(4, weight_part)
    to_core = remote(wall.at[:, :, :, 1 - c], core_in, x_sem.at[4], x_sem.at[5], seq_of(x, z, y, 1 - c))
    to_core.start()

    def back(i):
        back_ref[at(i, 256), :] = dot(vg_ref[at(i, 256), :], wm[...], cb=1)

    loop(2, back)
    to_core.wait()

    def add_core(i):
        mine = wall[i, :, :, c].astype(F32)
        plane_out[i] = (mine + core_in[i].astype(F32)).astype(BF16)

    loop(4, add_core)
    keep = pltpu.make_async_copy(plane_out.at[x, :, y], plane_in.at[x, y], own_sem.at[4])
    keep.start()
    for i in range(1, 16):
        tx, ty = lax.rem(x + i // 4, 4), lax.rem(y + i % 4, 4)
        remote(plane_out.at[tx, :, ty], plane_in.at[x, y], x_sem.at[6], x_sem.at[7], seq_of(tx, z, ty, c)).start()

    loop(2, lambda i: back(i + 2))
    keep.wait()
    settle(s1.at[pl.ds(0, 60)], x_sem.at[7])
    settle(s1.at[pl.ds(0, 60)], x_sem.at[6])

    def add_plane(i):
        total = jnp.zeros((16, 512), F32)
        for j in range(16):
            total = total + plane_in[j // 4, j % 4, i].astype(F32)
        z_out[i] = total.astype(BF16)

    loop(4, add_plane)
    zz = z * 2 + dp
    keep = pltpu.make_async_copy(z_out.at[z], z_in.at[zz], own_sem.at[5])
    keep.start()
    for i in range(1, 8):
        tz = lax.rem(zz + i, 8)
        th = lax.div(tz, 2)
        remote(z_out.at[th], z_in.at[zz], x_sem.at[8], x_sem.at[9], seq_of(x, th, y, c), lax.rem(tz, 2)).start()

    left_swap.wait()

    def left_sum(b):
        lg_sum[b] = lg_own[b].astype(F32) + lg_other[b].astype(F32)

    loop(4, left_sum)
    left_out = pltpu.make_async_copy(lg_sum, lgrad_hbm, out_sem.at[0])
    left_out.start()

    right_swap.wait()

    def right_sum(i):
        for a in range(2):
            rg_sum[a, at(i, 128), :] = rg_own[a, at(i, 128), :].astype(F32) + rg_other[a, at(i, 128), :].astype(F32)

    loop(4, right_sum)
    right_out = pltpu.make_async_copy(rg_sum, rgrad_hbm, out_sem.at[1])
    right_out.start()

    arrived(3, s4, r4)

    def finish(i):
        for m in range(2):
            cols = slice(512 * m, 512 * m + 512)
            parts = deinterleave(unpack(r4[at(i, 16), :, 256 * m : 256 * m + 256]))
            for a in range(2):
                rows = pl.ds(pl.multiple_of(512 * a + i * 64, 64), 64)
                second = parts[a].reshape(64, 512)
                mixed_ref[rows, cols] = (x_ref[rows, cols].astype(F32) * second).astype(BF16)
                igrad_ref[rows, cols] = (u_ref[rows, cols].astype(F32) * second + back_ref[rows, cols]).astype(BF16)

    loop(8, finish)
    mixed_out = pltpu.make_async_copy(mixed_ref, mixed_hbm, out_sem.at[2])
    mixed_out.start()
    igrad_out = pltpu.make_async_copy(igrad_ref, igrad_hbm, out_sem.at[3])
    igrad_out.start()

    keep.wait()
    settle(z_in.at[pl.ds(0, 7)], x_sem.at[9])
    settle(z_in.at[pl.ds(0, 7)], x_sem.at[8])
    total = jnp.zeros((16, 512), F32)
    for j in range(8):
        total = total + z_in[j].astype(F32)
    for m in range(2):
        for h in range(2):
            wgrad_ref[:, 512 * m + 256 * h : 512 * m + 256 * h + 256] = total[8 * h : 8 * h + 8, 256 * m : 256 * m + 256]

    sent(0, s1)
    sent(1, s2)
    sent(2, s3)
    sent(3, s4)
    left_out.wait()
    right_out.wait()
    mixed_out.wait()
    igrad_out.wait()


def body(inputs, cotangent, w_value, right_factor, left_factor):
    vmem = pl.BlockSpec(memory_space=pltpu.VMEM)
    hbm = pl.BlockSpec(memory_space=pl.ANY)

    def scratch(*shape, dtype=BF16):
        return pltpu.VMEM(shape, dtype)

    square = scratch(1024, 1024)
    wire = scratch(N, 16, 512)
    mixed, igrad, rgrad, lgrad, wgrad = pl.pallas_call(
        mixer,
        name="mixer",
        out_shape=(
            jax.ShapeDtypeStruct((1024, 1024), BF16),
            jax.ShapeDtypeStruct((1024, 1024), BF16),
            jax.ShapeDtypeStruct((2, 512, 512), F32),
            jax.ShapeDtypeStruct((4, 256, 256), F32),
            jax.ShapeDtypeStruct((8, 1024), F32),
        ),
        in_specs=[vmem] * 5,
        out_specs=(hbm, hbm, hbm, hbm, vmem),
        scratch_shapes=[wire] * 8
        + [scratch(4, 4, 4, 2, 16, 512)]
        + [square] * 9
        + [square, scratch(1024, 256), scratch(4, 256, 256), scratch(4, 256, 256), scratch(4, 256, 256, dtype=F32)]
        + [scratch(2, 512, 512), scratch(2, 512, 512), scratch(2, 512, 512, dtype=F32)]
        + [scratch(4, 4, 4, 16, 512)] * 3
        + [scratch(4, 16, 512), scratch(8, 16, 512), scratch(1024, 1024, dtype=F32), square, square]
        + [pltpu.SemaphoreType.DMA((4,))] * 2
        + [pltpu.SemaphoreType.DMA((6,)), pltpu.SemaphoreType.DMA((8,)), pltpu.SemaphoreType.DMA((10,)), pltpu.SemaphoreType.DMA((4,))],
        compiler_params=pltpu.CompilerParams(has_side_effects=True, vmem_limit_bytes=62 << 20),
        cost_estimate=pl.CostEstimate(flops=26_000_000_000, bytes_accessed=14_000_000, transcendentals=0),
    )(inputs.reshape(1024, 1024), cotangent.reshape(1024, 1024), w_value, right_factor, left_factor)
    shape = inputs.shape
    return mixed.reshape(shape), igrad.reshape(shape), rgrad, lgrad, wgrad


def solution(mesh):
    placed = (
        P("dp", "seq", None),
        P("dp", "seq", None),
        P("seq", None),
        P("seq", None, None),
        P("seq", None, None),
    )
    return jax.shard_map(
        body,
        mesh=mesh,
        in_specs=placed,
        out_specs=(
            P("dp", "seq", None),
            P("dp", "seq", None),
            P("seq", None, None),
            P("seq", None, None),
            P("seq", None),
        ),
        check_vma=False,
    )
```

time: 1210 us -> 259 us (0.21)
  waiting for transfers between devices: 859 us -> 0 us
  Pallas kernels: 0 us -> 249 us
  blocking collectives: 244 us -> 0 us
  local copies, waits for them, and re-layouts: 49.6 us -> 9.13 us
  matrix products: 34.1 us -> 0 us
  between operations: 13.9 us -> 0.65 us
    unnamed x4 -> x0, waiting for transfers between devices: 687 us -> none
    pallas_call x0 -> x1, Pallas kernels: none -> 249 us  [body(): pl.pallas_call(mixer, name='mixer', out_shape=(jax.ShapeDtypeStruct((1024...]
    all_to_all x4 -> x0, blocking collectives: 232 us -> none  [the longest x2 120 us: to_blocks(): return lax.all_to_all(array, 'seq', split_axis=2, concat_axis=1, tiled=True)]
    psum x1 -> x0, waiting for transfers between devices: 87.2 us -> none  [body(): lax.psum((right_grad, left_grad, whole_grad), 'dp')]
    all_gather x1 -> x0, waiting for transfers between devices: 84.5 us -> none  [body(): whole_weight = lax.all_gather(w_value, 'seq', axis=0, tiled=True)]
    dot_general x9 -> x0, matrix products: 34.1 us -> none  [the longest x1 7.15 us: body(): lax.dot_general(grad_rows_flat, whole_weight, (((1,), (1,)), ((), ())), p...]
    convert_element_type x5 -> x0, local copies, waits for them, and re-layouts: 22.2 us -> none  [the longest x2 8.23 us: body(): mixed = (inputs32 * second.astype(jnp.float32)).astype(jnp.bfloat16)]
  transfers between devices with their start and end apart: 3 -> 0, of which waited for: 3 -> 0; matrix products, arithmetic and copies ran while one was open for 1% -> 0% of each run, Pallas kernels for 0% -> 0%
where the time goes in v1:
time: 259 us
  Pallas kernels  249 us (96%)
  local copies, waits for them, and re-layouts  9.13 us (4%)
    pallas_call x1, Pallas kernels, body(): pl.pallas_call(mixer, name='mixer', out_shape=(jax.ShapeDtypeStruct((1024...  249 us
    unnamed x13, local copies, waits for them, and re-layouts  9.13 us

profile of v1, /device:TPU:1, one launch (start us, length us, event | category | flops | bytes accessed | tf_op | source)
XLA Modules:
  0.0 258.5 jit_solution(15295474000149940750)
XLA Ops:
  0.6 248.8 %mixer.1 = (bf16[1024,1024]{1,0:T(8,128)(2,1)}, bf16[1024,1024]{1,0:T(8,128)(2,1)}, f32[2,512,512]{2,1,0:T(8,128)}, f32[4,256,256]{2,1,0:T(8,128)}, f32[8,1024]{1,0:T(8,128)}) custom-call(bf16[1024,1024]{1,0:T(8,128)(2,1)} %bitcast.6, bf16[1024,1024]{1,0:T(8,128)(2,1)} %bitcast.7, bf16[8,1024]{1,0:T(8,128)(2,1)} %w_ref.1, bf16[2,512,512]{2,1,0:T(8,128)(2,1)} %r_ref.1, ...), custom_call_target="tpu_custom_call" | custom-call | flops 25999998976 | bytes 14000000 | tf_op jit(solution)/shard_map/mixer/pallas_call | solution.py:372
  249.4 0.0 copy-start.1
  249.4 3.2 %copy.15 = bf16[1,1024,1024]{2,1,0:T(8,128)(2,1)} copy(bf16[1,1024,1024]{2,1,0:T(8,128)(2,1)} %bitcast.5) | data formatting | bytes 4194304
  252.6 0.0 copy-done.1
  252.6 0.0 copy-start
  252.6 1.3 copy.16
  254.0 1.0 copy-done
  255.0 0.0 copy-start.2
  255.0 1.3 copy.17
  256.3 0.6 copy-done.2
  256.9 0.0 copy-start.3
  256.9 1.0 copy.18
  257.9 0.0 copy-done.3
  257.9 0.6 copy.19
Async XLA Ops:
  249.4 3.2 %copy-start.1 = (bf16[1024,1024]{1,0:T(8,128)(2,1)S(1)}, bf16[1024,1024]{1,0:T(8,128)(2,1)}, u32[]{:S(2)}) copy-start(bf16[1024,1024]{1,0:T(8,128)(2,1)} %get-tuple-element.11) | copy-start | bytes 6291460
  252.6 2.3 copy-start
  255.0 2.0 copy-start.2
  256.9 1.0 copy-start.3

commit v2 on v1

--- a/solution.py
+++ b/solution.py
@@ -60,13 +60,12 @@
 
 
 def mixer(
-    x_ref, u_ref, w_ref, r_ref, l_ref,
-    mixed_hbm, igrad_hbm, rgrad_hbm, lgrad_hbm, wgrad_ref,
-    s1, r1, s2, r2, s3, r3, s4, r4,
+    x_hbm, u_hbm, w_ref, r_hbm, l_hbm,
+    x_ref, u_ref, r4, back_ref, rg_own, rg_other, lg_own, lg_other, z_in,
+    r_ref, l_ref, s1, r1, s2, r2, s3, r3, s4,
     wall, wm, m_ref, mt_ref, t_ref, g_ref, f_ref, v_ref, fg_ref, vg_ref,
-    lg_big, lg_mid, lg_own, lg_other, lg_sum, rg_own, rg_other, rg_sum,
-    core_in, plane_out, plane_in, z_out, z_in, back_ref, mixed_ref, igrad_ref,
-    send_sem, recv_sem, own_sem, w_sem, x_sem, out_sem,
+    lg_big, lg_mid, core_in, plane_out, plane_in, z_out,
+    send_sem, recv_sem, own_sem, w_sem, x_sem, in_sem,
 ):
     me = lax.axis_index("seq")
     dp = lax.axis_index("dp")
@@ -100,6 +99,23 @@
     def sent(i, src):
         settle(src.at[pl.ds(0, N - 1)], send_sem.at[i])
 
+    def piece(j):
+        return lax.rem(lax.div(me, 8) + j, 16)
+
+    def load(j):
+        b0 = pl.multiple_of(piece(j) * 32, 32)
+        for a in range(2):
+            for src, dst in ((x_hbm, x_ref), (u_hbm, u_ref)):
+                pltpu.make_async_copy(
+                    src.at[a, pl.ds(b0, 32)], dst.at[pl.ds(512 * a + b0, 32)], in_sem.at[j]
+                ).start()
+
+    loop(16, load)
+    left_in = pltpu.make_async_copy(l_hbm, l_ref, in_sem.at[16])
+    left_in.start()
+    right_in = pltpu.make_async_copy(r_hbm, r_ref, in_sem.at[17])
+    right_in.start()
+
     for m in range(2):
         rows = w_ref[:, 512 * m : 512 * m + 512].astype(F32).reshape(1, 8, 512)
         wall[x, z, y, c, :, 256 * m : 256 * m + 256] = pack(rows).reshape(16, 256)
@@ -114,7 +130,9 @@
 
     spread(0, wall.at[x, z, y, c], [seq_of(x, lax.rem(z + i, 4), y, c) for i in (1, 2, 3)])
 
-    def second_grad(i):
+    def second_grad(j):
+        i = piece(j)
+        settle(s1.at[pl.ds(0, 16)], in_sem.at[j])
         a0, a1 = at(i, 32), pl.ds(pl.multiple_of(512 + i * 32, 32), 32)
         for m in range(2):
             cols = slice(512 * m, 512 * m + 512)
@@ -123,8 +141,17 @@
             both = interleave(t0.reshape(4, 8, 512), t1.reshape(4, 8, 512))
             s1[at(i, 8), :, 256 * m : 256 * m + 256] = pack(both)
 
+        def send(k):
+            d = 8 * i + lax.rem(me + k, 8)
+
+            @pl.when(d != me)
+            def _():
+                remote(s1.at[d], r1.at[me], send_sem.at[0], recv_sem.at[0], d).start()
+
+        loop(8, send)
+
     loop(16, second_grad)
-    exchange(0, s1, r1)
+    pltpu.make_async_copy(s1.at[me], r1.at[me], own_sem.at[0]).start()
 
     def widen(b):
         select = (
@@ -151,6 +178,7 @@
 
     spread_done(0, wall.at[0, pl.ds(0, 3), 0, 0])
     spread(1, wall.at[x, :, y, c], [seq_of(lax.rem(x + i, 4), z, y, c) for i in (1, 2, 3)])
+    left_in.wait()
     build(True, mt_ref)
     spread_done(1, wall.at[pl.ds(0, 3), :, 0, 0])
     spread(2, wall.at[:, :, y, c], [seq_of(x, z, lax.rem(y + i, 4), c) for i in (1, 2, 3)])
@@ -179,6 +207,7 @@
             both = interleave(t0.reshape(32, 8, 512), t1.reshape(32, 8, 512))
             s2[at(i, 64), :, 256 * m : 256 * m + 256] = pack(both)
 
+    right_in.wait()
     loop(2, first)
     exchange(1, s2, r2)
 
@@ -303,61 +332,67 @@
         th = lax.div(tz, 2)
         remote(z_out.at[th], z_in.at[zz], x_sem.at[8], x_sem.at[9], seq_of(x, th, y, c), lax.rem(tz, 2)).start()
 
+    keep.wait()
+    settle(s1.at[pl.ds(0, 7)], x_sem.at[9])
+    settle(s1.at[pl.ds(0, 7)], x_sem.at[8])
+    sent(0, s1)
+    sent(1, s2)
+    sent(2, s3)
     left_swap.wait()
-
-    def left_sum(b):
-        lg_sum[b] = lg_own[b].astype(F32) + lg_other[b].astype(F32)
-
-    loop(4, left_sum)
-    left_out = pltpu.make_async_copy(lg_sum, lgrad_hbm, out_sem.at[0])
-    left_out.start()
-
     right_swap.wait()
-
-    def right_sum(i):
+    sent(3, s4)
+    arrived(3, s4, r4)
+
+
+def finish(
+    x_ref, u_ref, r4, back_ref, rg_own, rg_other, lg_own, lg_other, z_in,
+    mixed_hbm, igrad_hbm, rgrad_hbm, lgrad_hbm, wgrad_hbm,
+    mixed, igrad, rgrad, lgrad, wgrad, sem,
+):
+    def moves(i):
+        b = at(i, 64)
+        return (
+            pltpu.make_async_copy(mixed.at[:, b], mixed_hbm.at[:, b], sem.at[0, i]),
+            pltpu.make_async_copy(igrad.at[:, b], igrad_hbm.at[:, b], sem.at[1, i]),
+            pltpu.make_async_copy(rgrad.at[:, b], rgrad_hbm.at[:, b], sem.at[2, i]),
+            pltpu.make_async_copy(lgrad.at[:, at(i, 32)], lgrad_hbm.at[:, at(i, 32)], sem.at[3, i]),
+        )
+
+    def part(i):
+        b = at(i, 64)
         for a in range(2):
-            rg_sum[a, at(i, 128), :] = rg_own[a, at(i, 128), :].astype(F32) + rg_other[a, at(i, 128), :].astype(F32)
-
-    loop(4, right_sum)
-    right_out = pltpu.make_async_copy(rg_sum, rgrad_hbm, out_sem.at[1])
-    right_out.start()
-
-    arrived(3, s4, r4)
-
-    def finish(i):
+            rgrad[a, b, :] = rg_own[a, b, :].astype(F32) + rg_other[a, b, :].astype(F32)
         for m in range(2):
             cols = slice(512 * m, 512 * m + 512)
             parts = deinterleave(unpack(r4[at(i, 16), :, 256 * m : 256 * m + 256]))
             for a in range(2):
                 rows = pl.ds(pl.multiple_of(512 * a + i * 64, 64), 64)
                 second = parts[a].reshape(64, 512)
-                mixed_ref[rows, cols] = (x_ref[rows, cols].astype(F32) * second).astype(BF16)
-                igrad_ref[rows, cols] = (u_ref[rows, cols].astype(F32) * second + back_ref[rows, cols]).astype(BF16)
-
-    loop(8, finish)
-    mixed_out = pltpu.make_async_copy(mixed_ref, mixed_hbm, out_sem.at[2])
-    mixed_out.start()
-    igrad_out = pltpu.make_async_copy(igrad_ref, igrad_hbm, out_sem.at[3])
-    igrad_out.start()
-
-    keep.wait()
-    settle(z_in.at[pl.ds(0, 7)], x_sem.at[9])
-    settle(z_in.at[pl.ds(0, 7)], x_sem.at[8])
+                mixed[a, b, cols] = (x_ref[rows, cols].astype(F32) * second).astype(BF16)
+                igrad[a, b, cols] = (u_ref[rows, cols].astype(F32) * second + back_ref[rows, cols]).astype(BF16)
+        q = at(i, 32)
+        for k in range(4):
+            lgrad[k, q, :] = lg_own[k, q, :].astype(F32) + lg_other[k, q, :].astype(F32)
+        for move in moves(i):
+            move.start()
+
+    loop(8, part)
     total = jnp.zeros((16, 512), F32)
     for j in range(8):
         total = total + z_in[j].astype(F32)
     for m in range(2):
         for h in range(2):
-            wgrad_ref[:, 512 * m + 256 * h : 512 * m + 256 * h + 256] = total[8 * h : 8 * h + 8, 256 * m : 256 * m + 256]
-
-    sent(0, s1)
-    sent(1, s2)
-    sent(2, s3)
-    sent(3, s4)
-    left_out.wait()
-    right_out.wait()
-    mixed_out.wait()
-    igrad_out.wait()
+            to = 512 * m + 256 * h
+            wgrad[:, to : to + 256] = total[8 * h : 8 * h + 8, 256 * m : 256 * m + 256]
+    last = pltpu.make_async_copy(wgrad, wgrad_hbm, sem.at[4, 0])
+    last.start()
+
+    def ended(i):
+        for move in moves(i):
+            move.wait()
+
+    loop(8, ended)
+    last.wait()
 
 
 def body(inputs, cotangent, w_value, right_factor, left_factor):
@@ -367,32 +402,63 @@
     def scratch(*shape, dtype=BF16):
         return pltpu.VMEM(shape, dtype)
 
+    def array(*shape, dtype=BF16):
+        return jax.ShapeDtypeStruct(shape, dtype)
+
     square = scratch(1024, 1024)
     wire = scratch(N, 16, 512)
-    mixed, igrad, rgrad, lgrad, wgrad = pl.pallas_call(
+    x2, u2 = inputs.reshape(2, 512, 1024), cotangent.reshape(2, 512, 1024)
+    kept = pl.pallas_call(
         mixer,
         name="mixer",
         out_shape=(
-            jax.ShapeDtypeStruct((1024, 1024), BF16),
-            jax.ShapeDtypeStruct((1024, 1024), BF16),
-            jax.ShapeDtypeStruct((2, 512, 512), F32),
-            jax.ShapeDtypeStruct((4, 256, 256), F32),
-            jax.ShapeDtypeStruct((8, 1024), F32),
+            square,
+            square,
+            wire,
+            scratch(1024, 1024, dtype=F32),
+            scratch(2, 512, 512),
+            scratch(2, 512, 512),
+            scratch(4, 256, 256),
+            scratch(4, 256, 256),
+            scratch(8, 16, 512),
         ),
-        in_specs=[vmem] * 5,
-        out_specs=(hbm, hbm, hbm, hbm, vmem),
-        scratch_shapes=[wire] * 8
+        in_specs=[hbm, hbm, vmem, hbm, hbm],
+        out_specs=(vmem,) * 9,
+        scratch_shapes=[scratch(2, 512, 512), scratch(4, 256, 256)]
+        + [wire] * 7
         + [scratch(4, 4, 4, 2, 16, 512)]
         + [square] * 9
-        + [square, scratch(1024, 256), scratch(4, 256, 256), scratch(4, 256, 256), scratch(4, 256, 256, dtype=F32)]
-        + [scratch(2, 512, 512), scratch(2, 512, 512), scratch(2, 512, 512, dtype=F32)]
+        + [square, scratch(1024, 256)]
         + [scratch(4, 4, 4, 16, 512)] * 3
-        + [scratch(4, 16, 512), scratch(8, 16, 512), scratch(1024, 1024, dtype=F32), square, square]
-        + [pltpu.SemaphoreType.DMA((4,))] * 2
-        + [pltpu.SemaphoreType.DMA((6,)), pltpu.SemaphoreType.DMA((8,)), pltpu.SemaphoreType.DMA((10,)), pltpu.SemaphoreType.DMA((4,))],
-        compiler_params=pltpu.CompilerParams(has_side_effects=True, vmem_limit_bytes=62 << 20),
+        + [scratch(4, 16, 512)]
+        + [pltpu.SemaphoreType.DMA((n,)) for n in (4, 4, 6, 8, 10, 18)],
+        compiler_params=pltpu.CompilerParams(has_side_effects=True, vmem_limit_bytes=48 << 20),
         cost_estimate=pl.CostEstimate(flops=26_000_000_000, bytes_accessed=14_000_000, transcendentals=0),
-    )(inputs.reshape(1024, 1024), cotangent.reshape(1024, 1024), w_value, right_factor, left_factor)
+    )(x2, u2, w_value, right_factor, left_factor)
+    kept = [pltpu.with_memory_space_constraint(k, pltpu.VMEM) for k in kept]
+    mixed, igrad, rgrad, lgrad, wgrad = pl.pallas_call(
+        finish,
+        name="finish",
+        out_shape=(
+            array(2, 512, 1024),
+            array(2, 512, 1024),
+            array(2, 512, 512, dtype=F32),
+            array(4, 256, 256, dtype=F32),
+            array(8, 1024, dtype=F32),
+        ),
+        in_specs=[vmem] * 9,
+        out_specs=(hbm,) * 5,
+        scratch_shapes=[
+            scratch(2, 512, 1024),
+            scratch(2, 512, 1024),
+            scratch(2, 512, 512, dtype=F32),
+            scratch(4, 256, 256, dtype=F32),
+            scratch(8, 1024, dtype=F32),
+            pltpu.SemaphoreType.DMA((5, 8)),
+        ],
+        compiler_params=pltpu.CompilerParams(vmem_limit_bytes=10 << 20),
+        cost_estimate=pl.CostEstimate(flops=10_000_000, bytes_accessed=7_000_000, transcendentals=0),
+    )(*kept)
     shape = inputs.shape
     return mixed.reshape(shape), igrad.reshape(shape), rgrad, lgrad, wgrad
 

time: 259 us -> 250 us (0.965)
  local copies, waits for them, and re-layouts: 9.13 us -> 0 us
    unnamed x13 -> x0, local copies, waits for them, and re-layouts: 9.13 us -> none
    pallas_call x1 -> x2, Pallas kernels: 249 us -> 247 us  [the longest x1 244 us: body(): pl.pallas_call(mixer, name='mixer', out_shape=(square, square, wire, scra...]
where the time goes in v2:
time: 250 us; the launch traced here: 248 us
  Pallas kernels  247 us (99%)
    pallas_call x1, Pallas kernels, body(): pl.pallas_call(mixer, name='mixer', out_shape=(square, square, wire, scra...  244 us

profile of v2, /device:TPU:1, one launch (start us, length us, event | category | flops | bytes accessed | tf_op | source)
XLA Modules:
  0.0 248.1 jit_solution(9782180555300352189)
XLA Ops:
  0.6 244.0 %mixer.1 = (bf16[1024,1024]{1,0:T(8,128)(2,1)S(1)}, bf16[1024,1024]{1,0:T(8,128)(2,1)S(1)}, bf16[128,16,512]{2,1,0:T(8,128)(2,1)S(1)}, f32[1024,1024]{1,0:T(8,12...) custom-call(bf16[2,512,1024]{2,1,0:T(8,128)(2,1)} %bitcast.4, ...), custom_call_target="tpu_custom_call" | custom-call | flops 25999998976 | bytes 14000000 | tf_op jit(solution)/shard_map/mixer/pallas_call | solution.py:411
  244.7 3.4 %finish.1 = (bf16[2,512,1024]{2,1,0:T(8,128)(2,1)}, bf16[2,512,1024]{2,1,0:T(8,128)(2,1)}, f32[2,512,512]{2,1,0:T(8,128)}, f32[4,256,256]{2,1,0:T(8,128)}, f32[8,1024]{1,0:T(8,128)}) custom-call(bf16[1024,1024]{1,0:T(8,128)(2,1)S(1)} %get-tuple-element.19.x_ref, bf16[1024,1024]{1,0:T(8,128)(2,1)S(1)} %get-tuple-element.20.u_ref, ...), custom_call_target="tpu_custom_call" | custom-call | flops 10000000 | bytes 7000000 | tf_op jit(solution)/shard_map/finish/pallas_call | solution.py:439

commit v3 on v2

--- a/solution.py
+++ b/solution.py
@@ -83,21 +83,27 @@
     def settle(ref, sem):
         pltpu.make_async_copy(ref, ref, sem).wait()
 
-    def exchange(i, src, dst):
-        pltpu.make_async_copy(src.at[me], dst.at[me], own_sem.at[i]).start()
+    def half(m):
+        return pl.ds(256 * m, 256)
+
+    def exchange(i, m, src, dst):
+        pltpu.make_async_copy(src.at[me, :, half(m)], dst.at[me, :, half(m)], own_sem.at[2 * i + m]).start()
 
         def send(k):
             d = lax.rem(me + k + 1, N)
-            remote(src.at[d], dst.at[me], send_sem.at[i], recv_sem.at[i], d).start()
+            remote(
+                src.at[d, :, half(m)], dst.at[me, :, half(m)], send_sem.at[2 * i + m], recv_sem.at[2 * i + m], d
+            ).start()
 
         loop(N - 1, send)
 
-    def arrived(i, src, dst):
-        pltpu.make_async_copy(src.at[me], dst.at[me], own_sem.at[i]).wait()
-        settle(dst.at[pl.ds(0, N - 1)], recv_sem.at[i])
+    def arrived(i, m, src, dst):
+        pltpu.make_async_copy(src.at[me, :, half(m)], dst.at[me, :, half(m)], own_sem.at[2 * i + m]).wait()
+        settle(dst.at[pl.ds(0, N - 1), :, half(m)], recv_sem.at[2 * i + m])
 
     def sent(i, src):
-        settle(src.at[pl.ds(0, N - 1)], send_sem.at[i])
+        for m in range(2):
+            settle(src.at[pl.ds(0, N - 1), :, half(m)], send_sem.at[2 * i + m])
 
     def piece(j):
         return lax.rem(lax.div(me, 8) + j, 16)
@@ -146,12 +152,13 @@
 
             @pl.when(d != me)
             def _():
-                remote(s1.at[d], r1.at[me], send_sem.at[0], recv_sem.at[0], d).start()
+                remote(s1.at[d, :, half(0)], r1.at[me, :, half(0)], send_sem.at[0], recv_sem.at[0], d).start()
 
         loop(8, send)
 
     loop(16, second_grad)
-    pltpu.make_async_copy(s1.at[me], r1.at[me], own_sem.at[0]).start()
+    pltpu.make_async_copy(s1.at[me, :, half(0)], r1.at[me, :, half(0)], own_sem.at[0]).start()
+    exchange(0, 1, s1, r1)
 
     def widen(b):
         select = (
@@ -176,15 +183,53 @@
 
         loop(4, rows)
 
+    def unpack_cols(src, dst, m):
+        def step(i):
+            part = unpack(src[at(i, 16), :, 256 * m : 256 * m + 256])
+            dst[at(i, 128), 512 * m : 512 * m + 512] = part.reshape(128, 512).astype(BF16)
+
+        loop(8, step)
+
+    def columns_product(big, cols_ref, out, m):
+        def step(i):
+            t = dot(big[at(i, 256), :], cols_ref[:, 512 * m : 512 * m + 512])
+            out[at(i, 32), :, 256 * m : 256 * m + 256] = pack(t.reshape(32, 8, 512))
+
+        loop(4, step)
+
+    def first_grad_columns(m):
+        arrived(0, m, s1, r1)
+        unpack_cols(r1, g_ref, m)
+        columns_product(mt_ref, g_ref, s3, m)
+        exchange(2, m, s3, r3)
+
+    def second_columns(m):
+        arrived(1, m, s2, r2)
+        unpack_cols(r2, f_ref, m)
+        columns_product(m_ref, f_ref, s4, m)
+        exchange(3, m, s4, r4)
+
+    def first_grad(m):
+        arrived(2, m, s3, r3)
+
+        def step(i):
+            t0, t1 = deinterleave(unpack(r3[at(i, 16), :, 256 * m : 256 * m + 256]))
+            cols = slice(512 * m, 512 * m + 512)
+            fg_ref[at(i, 64), cols] = t0.reshape(64, 512).astype(BF16)
+            fg_ref[pl.ds(pl.multiple_of(512 + i * 64, 64), 64), cols] = t1.reshape(64, 512).astype(BF16)
+
+        loop(8, step)
+
     spread_done(0, wall.at[0, pl.ds(0, 3), 0, 0])
     spread(1, wall.at[x, :, y, c], [seq_of(lax.rem(x + i, 4), z, y, c) for i in (1, 2, 3)])
     left_in.wait()
     build(True, mt_ref)
     spread_done(1, wall.at[pl.ds(0, 3), :, 0, 0])
     spread(2, wall.at[:, :, y, c], [seq_of(x, z, lax.rem(y + i, 4), c) for i in (1, 2, 3)])
-    build(False, m_ref)
+    first_grad_columns(0)
     spread_done(2, wall.at[:, :, pl.ds(0, 3), 0])
     spread(3, wall.at[:, :, :, c], [seq_of(x, z, y, 1 - c)])
+    right_in.wait()
     spread_done(3, wall.at[:, :, :, 0])
 
     def unpack_weight(i):
@@ -199,43 +244,24 @@
 
     loop(4, value)
 
-    def first(i):
-        for m in range(2):
+    def first(m):
+        def step(i):
             cols = slice(512 * m, 512 * m + 512)
             t0 = dot(r_ref[0, at(i, 256), :], v_ref[0:512, cols])
             t1 = dot(r_ref[1, at(i, 256), :], v_ref[512:1024, cols])
             both = interleave(t0.reshape(32, 8, 512), t1.reshape(32, 8, 512))
             s2[at(i, 64), :, 256 * m : 256 * m + 256] = pack(both)
 
-    right_in.wait()
-    loop(2, first)
-    exchange(1, s2, r2)
-
-    def unpack_all(src, dst):
-        def step(i):
-            for m in range(2):
-                part = src[at(i, 16), :, 256 * m : 256 * m + 256]
-                dst[at(i, 128), 512 * m : 512 * m + 512] = unpack(part).reshape(128, 512).astype(BF16)
-
-        loop(8, step)
-
-    def columns_product(big, cols_ref, out):
-        def step(i):
-            for m in range(2):
-                t = dot(big[at(i, 256), :], cols_ref[:, 512 * m : 512 * m + 512])
-                out[at(i, 32), :, 256 * m : 256 * m + 256] = pack(t.reshape(32, 8, 512))
-
-        loop(4, step)
-
-    arrived(0, s1, r1)
-    unpack_all(r1, g_ref)
-    columns_product(mt_ref, g_ref, s3)
-    exchange(2, s3, r3)
-
-    arrived(1, s2, r2)
-    unpack_all(r2, f_ref)
-    columns_product(m_ref, f_ref, s4)
-    exchange(3, s4, r4)
+        loop(2, step)
+        exchange(1, m, s2, r2)
+
+    first(0)
+    first(1)
+    first_grad_columns(1)
+    build(False, m_ref)
+    first_grad(0)
+    second_columns(0)
+    second_columns(1)
 
     def left_all(i):
         rows = dot(g_ref[at(i, 256), :], f_ref[...], cb=1)
@@ -263,16 +289,7 @@
     left_swap = remote(lg_own, lg_other, x_sem.at[0], x_sem.at[1], me, 1 - dp)
     left_swap.start()
 
-    arrived(2, s3, r3)
-
-    def first_grad(i):
-        for m in range(2):
-            t0, t1 = deinterleave(unpack(r3[at(i, 16), :, 256 * m : 256 * m + 256]))
-            cols = slice(512 * m, 512 * m + 512)
-            fg_ref[at(i, 64), cols] = t0.reshape(64, 512).astype(BF16)
-            fg_ref[pl.ds(pl.multiple_of(512 + i * 64, 64), 64), cols] = t1.reshape(64, 512).astype(BF16)
-
-    loop(8, first_grad)
+    first_grad(1)
 
     def right_part(i):
         rg_own[i] = dot(fg_ref[at(i, 512), :], v_ref[at(i, 512), :], cb=1).astype(BF16)
@@ -306,7 +323,7 @@
         plane_out[i] = (mine + core_in[i].astype(F32)).astype(BF16)
 
     loop(4, add_core)
-    keep = pltpu.make_async_copy(plane_out.at[x, :, y], plane_in.at[x, y], own_sem.at[4])
+    keep = pltpu.make_async_copy(plane_out.at[x, :, y], plane_in.at[x, y], own_sem.at[8])
     keep.start()
     for i in range(1, 16):
         tx, ty = lax.rem(x + i // 4, 4), lax.rem(y + i % 4, 4)
@@ -325,7 +342,7 @@
 
     loop(4, add_plane)
     zz = z * 2 + dp
-    keep = pltpu.make_async_copy(z_out.at[z], z_in.at[zz], own_sem.at[5])
+    keep = pltpu.make_async_copy(z_out.at[z], z_in.at[zz], own_sem.at[9])
     keep.start()
     for i in range(1, 8):
         tz = lax.rem(zz + i, 8)
@@ -341,7 +358,8 @@
     left_swap.wait()
     right_swap.wait()
     sent(3, s4)
-    arrived(3, s4, r4)
+    arrived(3, 0, s4, r4)
+    arrived(3, 1, s4, r4)
 
 
 def finish(
@@ -431,7 +449,7 @@
         + [square, scratch(1024, 256)]
         + [scratch(4, 4, 4, 16, 512)] * 3
         + [scratch(4, 16, 512)]
-        + [pltpu.SemaphoreType.DMA((n,)) for n in (4, 4, 6, 8, 10, 18)],
+        + [pltpu.SemaphoreType.DMA((n,)) for n in (8, 8, 10, 8, 10, 18)],
         compiler_params=pltpu.CompilerParams(has_side_effects=True, vmem_limit_bytes=48 << 20),
         cost_estimate=pl.CostEstimate(flops=26_000_000_000, bytes_accessed=14_000_000, transcendentals=0),
     )(x2, u2, w_value, right_factor, left_factor)

time: 250 us -> 249 us (level); the launches traced: 248 us -> 244 us
  Pallas kernels: 247 us -> 243 us
    pallas_call x1, Pallas kernels: 244 us -> 240 us  [body(): pl.pallas_call(mixer, name='mixer', out_shape=(square, square, wire, scra...]
where the time goes in v3:
time: 249 us; the launch traced here: 244 us
  Pallas kernels  243 us (98%)
    pallas_call x1, Pallas kernels, body(): pl.pallas_call(mixer, name='mixer', out_shape=(square, square, wire, scra...  240 us

profile of v3, /device:TPU:1, one launch (start us, length us, event | category | flops | bytes accessed | tf_op | source)
XLA Modules:
  0.0 244.1 jit_solution(1744327116896406223)
XLA Ops:
  0.6 240.1 %mixer.1 = (bf16[1024,1024]{1,0:T(8,128)(2,1)S(1)}, bf16[1024,1024]{1,0:T(8,128)(2,1)S(1)}, bf16[128,16,512]{2,1,0:T(8,128)(2,1)S(1)}, f32[1024,1024]{1,0:T(8,12...) custom-call(bf16[2,512,1024]{2,1,0:T(8,128)(2,1)} %bitcast.4, ...), custom_call_target="tpu_custom_call" | custom-call | flops 25999998976 | bytes 14000000 | tf_op jit(solution)/shard_map/mixer/pallas_call | solution.py:429
  240.7 3.4 %finish.1 = (bf16[2,512,1024]{2,1,0:T(8,128)(2,1)}, bf16[2,512,1024]{2,1,0:T(8,128)(2,1)}, f32[2,512,512]{2,1,0:T(8,128)}, f32[4,256,256]{2,1,0:T(8,128)}, f32[8,1024]{1,0:T(8,128)}) custom-call(bf16[1024,1024]{1,0:T(8,128)(2,1)S(1)} %get-tuple-element.19.x_ref, bf16[1024,1024]{1,0:T(8,128)(2,1)S(1)} %get-tuple-element.20.u_ref, ...), custom_call_target="tpu_custom_call" | custom-call | flops 10000000 | bytes 7000000 | tf_op jit(solution)/shard_map/finish/pallas_call | solution.py:457

commit v4 on v3

--- a/solution.py
+++ b/solution.py
@@ -59,12 +59,22 @@
     return pl.ds(pl.multiple_of(i * size, size), size)
 
 
+def results(i, m, x_ref, u_ref, r4, back_ref, mixed, igrad):
+    parts = deinterleave(unpack(r4[at(i, 16), :, 256 * m : 256 * m + 256]))
+    cols = slice(512 * m, 512 * m + 512)
+    for a in range(2):
+        rows = pl.ds(pl.multiple_of(512 * a + i * 64, 64), 64)
+        second = parts[a].reshape(64, 512)
+        mixed[a, at(i, 64), :] = (x_ref[rows, cols].astype(F32) * second).astype(BF16)
+        igrad[a, at(i, 64), :] = (u_ref[rows, cols].astype(F32) * second + back_ref[rows, cols]).astype(BF16)
+
+
 def mixer(
     x_hbm, u_hbm, w_ref, r_hbm, l_hbm,
-    x_ref, u_ref, r4, back_ref, rg_own, rg_other, lg_own, lg_other, z_in,
+    x_ref, u_ref, r4, back_ref, rg_own, rg_other, lg_own, lg_other, z_in, mixed_0, igrad_0,
     r_ref, l_ref, s1, r1, s2, r2, s3, r3, s4,
     wall, wm, m_ref, mt_ref, t_ref, g_ref, f_ref, v_ref, fg_ref, vg_ref,
-    lg_big, lg_mid, core_in, plane_out, plane_in, z_out,
+    lg_mid, core_in, plane_out, plane_in, z_out,
     send_sem, recv_sem, own_sem, w_sem, x_sem, in_sem,
 ):
     me = lax.axis_index("seq")
@@ -122,19 +132,14 @@
     right_in = pltpu.make_async_copy(r_hbm, r_ref, in_sem.at[17])
     right_in.start()
 
-    for m in range(2):
-        rows = w_ref[:, 512 * m : 512 * m + 512].astype(F32).reshape(1, 8, 512)
-        wall[x, z, y, c, :, 256 * m : 256 * m + 256] = pack(rows).reshape(16, 256)
-
-    def spread(phase, block, targets):
-        for t in targets:
-            remote(block, block, w_sem.at[2 * phase], w_sem.at[2 * phase + 1], t).start()
-
-    def spread_done(phase, like):
-        settle(like, w_sem.at[2 * phase + 1])
-        settle(like, w_sem.at[2 * phase])
-
-    spread(0, wall.at[x, z, y, c], [seq_of(x, lax.rem(z + i, 4), y, c) for i in (1, 2, 3)])
+    ready = pltpu.get_barrier_semaphore()
+
+    def greet(group, target):
+        pl.semaphore_signal(ready, inc=1, device_id=(group, target), device_id_type=MESH)
+
+    loop(N - 1, lambda k: greet(dp, lax.rem(me + k + 1, N)))
+    for i in range(4):
+        greet(1 - dp, seq_of(x, lax.rem(z + i, 4), y, c))
 
     def second_grad(j):
         i = piece(j)
@@ -147,8 +152,9 @@
             both = interleave(t0.reshape(4, 8, 512), t1.reshape(4, 8, 512))
             s1[at(i, 8), :, 256 * m : 256 * m + 256] = pack(both)
 
+    def second_grad_out(j):
         def send(k):
-            d = 8 * i + lax.rem(me + k, 8)
+            d = 8 * piece(j) + lax.rem(me + k, 8)
 
             @pl.when(d != me)
             def _():
@@ -156,7 +162,29 @@
 
         loop(8, send)
 
-    loop(16, second_grad)
+    for m in range(2):
+        rows = w_ref[:, 512 * m : 512 * m + 512].astype(F32).reshape(1, 8, 512)
+        wall[x, z, y, c, :, 256 * m : 256 * m + 256] = pack(rows).reshape(16, 256)
+
+    def spread(phase, block, targets):
+        for t in targets:
+            remote(block, block, w_sem.at[2 * phase], w_sem.at[2 * phase + 1], t).start()
+
+    def spread_done(phase, like):
+        settle(like, w_sem.at[2 * phase + 1])
+        settle(like, w_sem.at[2 * phase])
+
+
+    loop(4, lambda j: second_grad(j))
+    pl.semaphore_wait(ready, N + 3)
+    spread(0, wall.at[x, z, y, c], [seq_of(x, lax.rem(z + i, 4), y, c) for i in (1, 2, 3)])
+
+    def ahead(j):
+        second_grad_out(j)
+        second_grad(j + 4)
+
+    loop(12, ahead)
+    loop(4, lambda j: second_grad_out(j + 12))
     pltpu.make_async_copy(s1.at[me, :, half(0)], r1.at[me, :, half(0)], own_sem.at[0]).start()
     exchange(0, 1, s1, r1)
 
@@ -267,7 +295,7 @@
         rows = dot(g_ref[at(i, 256), :], f_ref[...], cb=1)
         row = lax.broadcasted_iota(jnp.int32, (256, 1024), 0)
         col = lax.broadcasted_iota(jnp.int32, (256, 1024), 1)
-        lg_big[at(i, 256), :] = jnp.where(lax.rem(row, 4) == lax.rem(col, 4), rows, 0.0).astype(BF16)
+        t_ref[at(i, 256), :] = jnp.where(lax.rem(row, 4) == lax.rem(col, 4), rows, 0.0).astype(BF16)
 
     loop(4, left_all)
 
@@ -275,7 +303,7 @@
         c_row = lax.broadcasted_iota(jnp.int32, (1024, 256), 0)
         c_col = lax.broadcasted_iota(jnp.int32, (1024, 256), 1)
         narrow = (lax.div(c_row, 4) == c_col).astype(F32).astype(BF16)
-        lg_mid[at(i, 256), :] = dot(lg_big[at(i, 256), :], narrow).astype(BF16)
+        lg_mid[at(i, 256), :] = dot(t_ref[at(i, 256), :], narrow).astype(BF16)
 
     loop(4, left_narrow)
 
@@ -348,6 +376,13 @@
         tz = lax.rem(zz + i, 8)
         th = lax.div(tz, 2)
         remote(z_out.at[th], z_in.at[zz], x_sem.at[8], x_sem.at[9], seq_of(x, th, y, c), lax.rem(tz, 2)).start()
+
+    arrived(3, 0, s4, r4)
+
+    def results_0(i):
+        results(i, 0, x_ref, u_ref, r4, back_ref, mixed_0, igrad_0)
+
+    loop(8, results_0)
 
     keep.wait()
     settle(s1.at[pl.ds(0, 7)], x_sem.at[9])
@@ -358,39 +393,37 @@
     left_swap.wait()
     right_swap.wait()
     sent(3, s4)
-    arrived(3, 0, s4, r4)
     arrived(3, 1, s4, r4)
 
 
 def finish(
-    x_ref, u_ref, r4, back_ref, rg_own, rg_other, lg_own, lg_other, z_in,
+    x_ref, u_ref, r4, back_ref, rg_own, rg_other, lg_own, lg_other, z_in, mixed_0, igrad_0,
     mixed_hbm, igrad_hbm, rgrad_hbm, lgrad_hbm, wgrad_hbm,
-    mixed, igrad, rgrad, lgrad, wgrad, sem,
+    mixed_1, igrad_1, rgrad, lgrad, wgrad, sem,
 ):
     def moves(i):
-        b = at(i, 64)
+        b, q = at(i, 64), at(i, 32)
         return (
-            pltpu.make_async_copy(mixed.at[:, b], mixed_hbm.at[:, b], sem.at[0, i]),
-            pltpu.make_async_copy(igrad.at[:, b], igrad_hbm.at[:, b], sem.at[1, i]),
+            pltpu.make_async_copy(mixed_1.at[:, b], mixed_hbm.at[:, b, pl.ds(512, 512)], sem.at[0, i]),
+            pltpu.make_async_copy(igrad_1.at[:, b], igrad_hbm.at[:, b, pl.ds(512, 512)], sem.at[1, i]),
             pltpu.make_async_copy(rgrad.at[:, b], rgrad_hbm.at[:, b], sem.at[2, i]),
-            pltpu.make_async_copy(lgrad.at[:, at(i, 32)], lgrad_hbm.at[:, at(i, 32)], sem.at[3, i]),
+            pltpu.make_async_copy(lgrad.at[:, q], lgrad_hbm.at[:, q], sem.at[3, i]),
         )
 
+    early = (
+        pltpu.make_async_copy(mixed_0, mixed_hbm.at[:, :, pl.ds(0, 512)], sem.at[4, 1]),
+        pltpu.make_async_copy(igrad_0, igrad_hbm.at[:, :, pl.ds(0, 512)], sem.at[4, 2]),
+    )
+    for move in early:
+        move.start()
+
     def part(i):
-        b = at(i, 64)
+        b, q = at(i, 64), at(i, 32)
         for a in range(2):
             rgrad[a, b, :] = rg_own[a, b, :].astype(F32) + rg_other[a, b, :].astype(F32)
-        for m in range(2):
-            cols = slice(512 * m, 512 * m + 512)
-            parts = deinterleave(unpack(r4[at(i, 16), :, 256 * m : 256 * m + 256]))
-            for a in range(2):
-                rows = pl.ds(pl.multiple_of(512 * a + i * 64, 64), 64)
-                second = parts[a].reshape(64, 512)
-                mixed[a, b, cols] = (x_ref[rows, cols].astype(F32) * second).astype(BF16)
-                igrad[a, b, cols] = (u_ref[rows, cols].astype(F32) * second + back_ref[rows, cols]).astype(BF16)
-        q = at(i, 32)
         for k in range(4):
             lgrad[k, q, :] = lg_own[k, q, :].astype(F32) + lg_other[k, q, :].astype(F32)
+        results(i, 1, x_ref, u_ref, r4, back_ref, mixed_1, igrad_1)
         for move in moves(i):
             move.start()
 
@@ -410,6 +443,8 @@
             move.wait()
 
     loop(8, ended)
+    for move in early:
+        move.wait()
     last.wait()
 
 
@@ -439,18 +474,22 @@
             scratch(4, 256, 256),
             scratch(4, 256, 256),
             scratch(8, 16, 512),
+            scratch(2, 512, 512),
+            scratch(2, 512, 512),
         ),
         in_specs=[hbm, hbm, vmem, hbm, hbm],
-        out_specs=(vmem,) * 9,
+        out_specs=(vmem,) * 11,
         scratch_shapes=[scratch(2, 512, 512), scratch(4, 256, 256)]
         + [wire] * 7
         + [scratch(4, 4, 4, 2, 16, 512)]
         + [square] * 9
-        + [square, scratch(1024, 256)]
+        + [scratch(1024, 256)]
         + [scratch(4, 4, 4, 16, 512)] * 3
         + [scratch(4, 16, 512)]
         + [pltpu.SemaphoreType.DMA((n,)) for n in (8, 8, 10, 8, 10, 18)],
-        compiler_params=pltpu.CompilerParams(has_side_effects=True, vmem_limit_bytes=48 << 20),
+        compiler_params=pltpu.CompilerParams(
+            collective_id=0, has_side_effects=True, vmem_limit_bytes=46 << 20
+        ),
         cost_estimate=pl.CostEstimate(flops=26_000_000_000, bytes_accessed=14_000_000, transcendentals=0),
     )(x2, u2, w_value, right_factor, left_factor)
     kept = [pltpu.with_memory_space_constraint(k, pltpu.VMEM) for k in kept]
@@ -464,11 +503,11 @@
             array(4, 256, 256, dtype=F32),
             array(8, 1024, dtype=F32),
         ),
-        in_specs=[vmem] * 9,
+        in_specs=[vmem] * 11,
         out_specs=(hbm,) * 5,
         scratch_shapes=[
-            scratch(2, 512, 1024),
-            scratch(2, 512, 1024),
+            scratch(2, 512, 512),
+            scratch(2, 512, 512),
             scratch(2, 512, 512, dtype=F32),
             scratch(4, 256, 256, dtype=F32),
             scratch(8, 1024, dtype=F32),

time: 249 us -> 242 us (0.972); the launches traced: 244 us -> 242 us
  no operation moved by 1% of the time
where the time goes in v4:
time: 242 us
  Pallas kernels  241 us (100%)
    pallas_call x1, Pallas kernels, body(): pl.pallas_call(mixer, name='mixer', out_shape=(square, square, wire, scra...  238 us

profile of v4, /device:TPU:1, one launch (start us, length us, event | category | flops | bytes accessed | tf_op | source)
XLA Modules:
  0.0 241.8 jit_solution(8839511228376127559)
XLA Ops:
  0.6 237.9 %mixer.1 = (bf16[1024,1024]{1,0:T(8,128)(2,1)S(1)}, bf16[1024,1024]{1,0:T(8,128)(2,1)S(1)}, bf16[128,16,512]{2,1,0:T(8,128)(2,1)S(1)}, f32[1024,1024]{1,0:T(8,12...) custom-call(bf16[2,512,1024]{2,1,0:T(8,128)(2,1)} %bitcast.4, ...), custom_call_target="tpu_custom_call" | custom-call | flops 25999998976 | bytes 14000000 | tf_op jit(solution)/shard_map/mixer/pallas_call | solution.py:464
  238.5 3.3 %finish.1 = (bf16[2,512,1024]{2,1,0:T(8,128)(2,1)}, bf16[2,512,1024]{2,1,0:T(8,128)(2,1)}, f32[2,512,512]{2,1,0:T(8,128)}, f32[4,256,256]{2,1,0:T(8,128)}, f32[8,1024]{1,0:T(8,128)}) custom-call(bf16[1024,1024]{1,0:T(8,128)(2,1)S(1)} %get-tuple-element.21.x_ref, bf16[1024,1024]{1,0:T(8,128)(2,1)S(1)} %get-tuple-element.22.u_ref, ...), custom_call_target="tpu_custom_call" | custom-call | flops 10000000 | bytes 7000000 | tf_op jit(solution)/shard_map/finish/pallas_call | solution.py:496

commit v5 on v4

--- a/solution.py
+++ b/solution.py
@@ -35,16 +35,43 @@
 
 def interleave(t0, t1):
     low = low_rows(t0.shape)
-    even = jnp.where(low, t0, pltpu.roll(t1, 4, 1))
-    odd = jnp.where(low, pltpu.roll(t0, 4, 1), t1)
-    return jnp.stack([even, odd], axis=1).reshape(2 * t0.shape[0], 8, t0.shape[2])
-
-
-def deinterleave(w):
-    pair = w.reshape(w.shape[0] // 2, 2, 8, w.shape[2])
-    even, odd = pair[:, 0], pair[:, 1]
-    low = low_rows(even.shape)
-    return jnp.where(low, even, pltpu.roll(odd, 4, 1)), jnp.where(low, pltpu.roll(even, 4, 1), odd)
+    return jnp.where(low, t0, pltpu.roll(t1, 4, 1)), jnp.where(low, pltpu.roll(t0, 4, 1), t1)
+
+
+def pairs(w):
+    pair = w.reshape(w.shape[0] // 2, 2, *w.shape[1:])
+    return pair[:, 0], pair[:, 1]
+
+
+def zipped(even, odd):
+    return jnp.stack([even, odd], axis=1).reshape(2 * even.shape[0], *even.shape[1:])
+
+
+def swap_middle(x):
+    row = lax.broadcasted_iota(jnp.int32, x.shape, 1)
+    up, down = pltpu.roll(x, 6, 1), pltpu.roll(x, 2, 1)
+    return jnp.where((row == 2) | (row == 3), up, jnp.where((row == 4) | (row == 5), down, x))
+
+
+def blocks(x):
+    e0, o0 = interleave(x[:, :, :128], x[:, :, 128:256])
+    e1, o1 = interleave(x[:, :, 256:384], x[:, :, 384:])
+    return zipped(jnp.concatenate([e0, e1], axis=1), jnp.concatenate([o0, o1], axis=1)).astype(BF16)
+
+
+def unblock(w):
+    even, odd = pairs(w.astype(F32))
+    c0, c1 = interleave(even[:, :8], odd[:, :8])
+    c2, c3 = interleave(even[:, 8:], odd[:, 8:])
+    return jnp.concatenate([c0, c1, c2, c3], axis=2)
+
+
+def to_owners(t0, t1):
+    return blocks(swap_middle(zipped(*interleave(t0, t1))))
+
+
+def from_owners(w):
+    return interleave(*pairs(swap_middle(unblock(w))))
 
 
 def loop(count, step):
@@ -60,7 +87,7 @@
 
 
 def results(i, m, x_ref, u_ref, r4, back_ref, mixed, igrad):
-    parts = deinterleave(unpack(r4[at(i, 16), :, 256 * m : 256 * m + 256]))
+    parts = from_owners(r4[at(i, 32), :, 128 * m : 128 * m + 128])
     cols = slice(512 * m, 512 * m + 512)
     for a in range(2):
         rows = pl.ds(pl.multiple_of(512 * a + i * 64, 64), 64)
@@ -71,7 +98,7 @@
 
 def mixer(
     x_hbm, u_hbm, w_ref, r_hbm, l_hbm,
-    x_ref, u_ref, r4, back_ref, rg_own, rg_other, lg_own, lg_other, z_in, mixed_0, igrad_0,
+    x_ref, u_ref, r4, back_ref, rg_own, rg_other, lg_all, z_in, mixed_0, igrad_0,
     r_ref, l_ref, s1, r1, s2, r2, s3, r3, s4,
     wall, wm, m_ref, mt_ref, t_ref, g_ref, f_ref, v_ref, fg_ref, vg_ref,
     lg_mid, core_in, plane_out, plane_in, z_out,
@@ -94,26 +121,40 @@
         pltpu.make_async_copy(ref, ref, sem).wait()
 
     def half(m):
-        return pl.ds(256 * m, 256)
+        return pl.ds(128 * m, 128)
+
+    pair_me, line_me = 2 * me + dp, dp * N + me
+
+    def to_owner(i, m, src, dst, q, k):
+        remote(
+            src.at[2 * q + k, :, half(m)], dst.at[line_me, :, half(m)], send_sem.at[2 * i + m], recv_sem.at[2 * i + m], q, k
+        ).start()
+
+    def to_source(i, m, src, dst, q, k):
+        remote(
+            src.at[k * N + q, :, half(m)], dst.at[pair_me, :, half(m)], send_sem.at[2 * i + m], recv_sem.at[2 * i + m], q, k
+        ).start()
+
+    def own(i, m, src, dst):
+        mine, there = (line_me, pair_me) if i >= 2 else (pair_me, line_me)
+        return pltpu.make_async_copy(src.at[mine, :, half(m)], dst.at[there, :, half(m)], own_sem.at[2 * i + m])
 
     def exchange(i, m, src, dst):
-        pltpu.make_async_copy(src.at[me, :, half(m)], dst.at[me, :, half(m)], own_sem.at[2 * i + m]).start()
+        own(i, m, src, dst).start()
 
         def send(k):
-            d = lax.rem(me + k + 1, N)
-            remote(
-                src.at[d, :, half(m)], dst.at[me, :, half(m)], send_sem.at[2 * i + m], recv_sem.at[2 * i + m], d
-            ).start()
-
-        loop(N - 1, send)
+            q, group = lax.rem(me + lax.div(k + 1, 2), N), lax.rem(dp + k + 1, 2)
+            (to_source if i >= 2 else to_owner)(i, m, src, dst, q, group)
+
+        loop(2 * N - 1, send)
 
     def arrived(i, m, src, dst):
-        pltpu.make_async_copy(src.at[me, :, half(m)], dst.at[me, :, half(m)], own_sem.at[2 * i + m]).wait()
-        settle(dst.at[pl.ds(0, N - 1), :, half(m)], recv_sem.at[2 * i + m])
+        own(i, m, src, dst).wait()
+        settle(dst.at[pl.ds(0, 2 * N - 1), :, half(m)], recv_sem.at[2 * i + m])
 
     def sent(i, src):
         for m in range(2):
-            settle(src.at[pl.ds(0, N - 1), :, half(m)], send_sem.at[2 * i + m])
+            settle(src.at[pl.ds(0, 2 * N - 1), :, half(m)], send_sem.at[2 * i + m])
 
     def piece(j):
         return lax.rem(lax.div(me, 8) + j, 16)
@@ -137,30 +178,28 @@
     def greet(group, target):
         pl.semaphore_signal(ready, inc=1, device_id=(group, target), device_id_type=MESH)
 
-    loop(N - 1, lambda k: greet(dp, lax.rem(me + k + 1, N)))
-    for i in range(4):
-        greet(1 - dp, seq_of(x, lax.rem(z + i, 4), y, c))
+    loop(2 * N - 1, lambda k: greet(lax.rem(dp + k + 1, 2), lax.rem(me + lax.div(k + 1, 2), N)))
 
     def second_grad(j):
         i = piece(j)
-        settle(s1.at[pl.ds(0, 16)], in_sem.at[j])
+        settle(s1.at[pl.ds(0, 32)], in_sem.at[j])
         a0, a1 = at(i, 32), pl.ds(pl.multiple_of(512 + i * 32, 32), 32)
         for m in range(2):
             cols = slice(512 * m, 512 * m + 512)
             t0 = x_ref[a0, cols].astype(F32) * u_ref[a0, cols].astype(F32)
             t1 = x_ref[a1, cols].astype(F32) * u_ref[a1, cols].astype(F32)
-            both = interleave(t0.reshape(4, 8, 512), t1.reshape(4, 8, 512))
-            s1[at(i, 8), :, 256 * m : 256 * m + 256] = pack(both)
+            s1[at(i, 16), :, 128 * m : 128 * m + 128] = to_owners(t0.reshape(4, 8, 512), t1.reshape(4, 8, 512))
 
     def second_grad_out(j):
         def send(k):
-            d = 8 * piece(j) + lax.rem(me + k, 8)
-
-            @pl.when(d != me)
+            d = 8 * piece(j) + lax.rem(me + lax.div(k, 2), 8)
+            group = lax.rem(dp + k, 2)
+
+            @pl.when((d != me) | (group != dp))
             def _():
-                remote(s1.at[d, :, half(0)], r1.at[me, :, half(0)], send_sem.at[0], recv_sem.at[0], d).start()
-
-        loop(8, send)
+                to_owner(0, 0, s1, r1, d, group)
+
+        loop(16, send)
 
     for m in range(2):
         rows = w_ref[:, 512 * m : 512 * m + 512].astype(F32).reshape(1, 8, 512)
@@ -176,7 +215,7 @@
 
 
     loop(4, lambda j: second_grad(j))
-    pl.semaphore_wait(ready, N + 3)
+    pl.semaphore_wait(ready, 2 * N - 1)
     spread(0, wall.at[x, z, y, c], [seq_of(x, lax.rem(z + i, 4), y, c) for i in (1, 2, 3)])
 
     def ahead(j):
@@ -185,45 +224,43 @@
 
     loop(12, ahead)
     loop(4, lambda j: second_grad_out(j + 12))
-    pltpu.make_async_copy(s1.at[me, :, half(0)], r1.at[me, :, half(0)], own_sem.at[0]).start()
+    own(0, 0, s1, r1).start()
     exchange(0, 1, s1, r1)
 
-    def widen(b):
-        select = (
-            lax.broadcasted_iota(jnp.int32, (256, 1024), 1)
-            == 4 * lax.broadcasted_iota(jnp.int32, (256, 1024), 0) + b
-        ).astype(F32).astype(BF16)
-        return select
+    def widen(j):
+        row = lax.broadcasted_iota(jnp.int32, (256, 512), 0)
+        col = lax.broadcasted_iota(jnp.int32, (256, 512), 1)
+        return (col == 2 * row + j).astype(F32).astype(BF16)
 
     def place(i):
-        row = lax.broadcasted_iota(jnp.int32, (256, 1024), 0) + i * 256
-        col = lax.broadcasted_iota(jnp.int32, (256, 1024), 1)
-        return (4 * lax.rem(col, 256) + lax.div(col, 256) == row).astype(F32).astype(BF16)
+        row = lax.broadcasted_iota(jnp.int32, (256, 512), 0) + i * 256
+        col = lax.broadcasted_iota(jnp.int32, (256, 512), 1)
+        return (2 * lax.rem(col, 256) + lax.div(col, 256) == row).astype(F32).astype(BF16)
 
     def build(transposed, out):
-        def wide(b):
-            t_ref[at(b, 256), :] = dot(l_ref[b], widen(b), ca=0 if transposed else 1).astype(BF16)
-
-        loop(4, wide)
+        def wide(j):
+            t_ref[at(j, 256), :] = dot(l_ref[2 * dp + j], widen(j), ca=0 if transposed else 1).astype(BF16)
+
+        loop(2, wide)
 
         def rows(i):
             out[at(i, 256), :] = dot(place(i), t_ref[...]).astype(BF16)
 
-        loop(4, rows)
+        loop(2, rows)
 
     def unpack_cols(src, dst, m):
         def step(i):
-            part = unpack(src[at(i, 16), :, 256 * m : 256 * m + 256])
+            part = unblock(src[at(i, 32), :, 128 * m : 128 * m + 128])
             dst[at(i, 128), 512 * m : 512 * m + 512] = part.reshape(128, 512).astype(BF16)
 
         loop(8, step)
 
     def columns_product(big, cols_ref, out, m):
-        def step(i):
-            t = dot(big[at(i, 256), :], cols_ref[:, 512 * m : 512 * m + 512])
-            out[at(i, 32), :, 256 * m : 256 * m + 256] = pack(t.reshape(32, 8, 512))
-
-        loop(4, step)
+        def step(s):
+            t = dot(big[...], cols_ref[at(s, 512), 512 * m : 512 * m + 512])
+            out[at(s, 128), :, 128 * m : 128 * m + 128] = blocks(t.reshape(64, 8, 512))
+
+        loop(2, step)
 
     def first_grad_columns(m):
         arrived(0, m, s1, r1)
@@ -241,7 +278,7 @@
         arrived(2, m, s3, r3)
 
         def step(i):
-            t0, t1 = deinterleave(unpack(r3[at(i, 16), :, 256 * m : 256 * m + 256]))
+            t0, t1 = from_owners(r3[at(i, 32), :, 128 * m : 128 * m + 128])
             cols = slice(512 * m, 512 * m + 512)
             fg_ref[at(i, 64), cols] = t0.reshape(64, 512).astype(BF16)
             fg_ref[pl.ds(pl.multiple_of(512 + i * 64, 64), 64), cols] = t1.reshape(64, 512).astype(BF16)
@@ -277,8 +314,7 @@
             cols = slice(512 * m, 512 * m + 512)
             t0 = dot(r_ref[0, at(i, 256), :], v_ref[0:512, cols])
             t1 = dot(r_ref[1, at(i, 256), :], v_ref[512:1024, cols])
-            both = interleave(t0.reshape(32, 8, 512), t1.reshape(32, 8, 512))
-            s2[at(i, 64), :, 256 * m : 256 * m + 256] = pack(both)
+            s2[at(i, 128), :, 128 * m : 128 * m + 128] = to_owners(t0.reshape(32, 8, 512), t1.reshape(32, 8, 512))
 
         loop(2, step)
         exchange(1, m, s2, r2)
@@ -292,29 +328,31 @@
     second_columns(1)
 
     def left_all(i):
-        rows = dot(g_ref[at(i, 256), :], f_ref[...], cb=1)
-        row = lax.broadcasted_iota(jnp.int32, (256, 1024), 0)
-        col = lax.broadcasted_iota(jnp.int32, (256, 1024), 1)
-        t_ref[at(i, 256), :] = jnp.where(lax.rem(row, 4) == lax.rem(col, 4), rows, 0.0).astype(BF16)
-
-    loop(4, left_all)
+        rows = dot(g_ref[at(i, 256), :], f_ref[0:512, :], cb=1)
+        rows = rows + dot(g_ref[pl.ds(pl.multiple_of(512 + i * 256, 256), 256), :], f_ref[512:1024, :], cb=1)
+        row = lax.broadcasted_iota(jnp.int32, (256, 512), 0)
+        col = lax.broadcasted_iota(jnp.int32, (256, 512), 1)
+        t_ref[at(i, 256), :] = jnp.where(lax.rem(row, 2) == lax.rem(col, 2), rows, 0.0).astype(BF16)
+
+    loop(2, left_all)
 
     def left_narrow(i):
-        c_row = lax.broadcasted_iota(jnp.int32, (1024, 256), 0)
-        c_col = lax.broadcasted_iota(jnp.int32, (1024, 256), 1)
-        narrow = (lax.div(c_row, 4) == c_col).astype(F32).astype(BF16)
+        row = lax.broadcasted_iota(jnp.int32, (512, 256), 0)
+        col = lax.broadcasted_iota(jnp.int32, (512, 256), 1)
+        narrow = (lax.div(row, 2) == col).astype(F32).astype(BF16)
         lg_mid[at(i, 256), :] = dot(t_ref[at(i, 256), :], narrow).astype(BF16)
 
-    loop(4, left_narrow)
-
-    def left_place(b):
-        row = lax.broadcasted_iota(jnp.int32, (256, 1024), 0)
-        col = lax.broadcasted_iota(jnp.int32, (256, 1024), 1)
-        take = (4 * row + b == col).astype(F32).astype(BF16)
-        lg_own[b] = dot(take, lg_mid[...]).astype(BF16)
-
-    loop(4, left_place)
-    left_swap = remote(lg_own, lg_other, x_sem.at[0], x_sem.at[1], me, 1 - dp)
+    loop(2, left_narrow)
+
+    def left_place(j):
+        row = lax.broadcasted_iota(jnp.int32, (256, 512), 0)
+        col = lax.broadcasted_iota(jnp.int32, (256, 512), 1)
+        take = (2 * row + j == col).astype(F32).astype(BF16)
+        lg_all[2 * dp + j] = dot(take, lg_mid[...]).astype(BF16)
+
+    loop(2, left_place)
+    done = lg_all.at[pl.ds(2 * dp, 2)]
+    left_swap = remote(done, done, x_sem.at[0], x_sem.at[1], me, 1 - dp)
     left_swap.start()
 
     first_grad(1)
@@ -359,8 +397,8 @@
 
     loop(2, lambda i: back(i + 2))
     keep.wait()
-    settle(s1.at[pl.ds(0, 60)], x_sem.at[7])
-    settle(s1.at[pl.ds(0, 60)], x_sem.at[6])
+    settle(s1.at[pl.ds(0, 120)], x_sem.at[7])
+    settle(s1.at[pl.ds(0, 120)], x_sem.at[6])
 
     def add_plane(i):
         total = jnp.zeros((16, 512), F32)
@@ -385,8 +423,8 @@
     loop(8, results_0)
 
     keep.wait()
-    settle(s1.at[pl.ds(0, 7)], x_sem.at[9])
-    settle(s1.at[pl.ds(0, 7)], x_sem.at[8])
+    settle(s1.at[pl.ds(0, 14)], x_sem.at[9])
+    settle(s1.at[pl.ds(0, 14)], x_sem.at[8])
     sent(0, s1)
     sent(1, s2)
     sent(2, s3)
@@ -397,7 +435,7 @@
 
 
 def finish(
-    x_ref, u_ref, r4, back_ref, rg_own, rg_other, lg_own, lg_other, z_in, mixed_0, igrad_0,
+    x_ref, u_ref, r4, back_ref, rg_own, rg_other, lg_all, z_in, mixed_0, igrad_0,
     mixed_hbm, igrad_hbm, rgrad_hbm, lgrad_hbm, wgrad_hbm,
     mixed_1, igrad_1, rgrad, lgrad, wgrad, sem,
 ):
@@ -422,7 +460,7 @@
         for a in range(2):
             rgrad[a, b, :] = rg_own[a, b, :].astype(F32) + rg_other[a, b, :].astype(F32)
         for k in range(4):
-            lgrad[k, q, :] = lg_own[k, q, :].astype(F32) + lg_other[k, q, :].astype(F32)
+            lgrad[k, q, :] = lg_all[k, q, :].astype(F32)
         results(i, 1, x_ref, u_ref, r4, back_ref, mixed_1, igrad_1)
         for move in moves(i):
             move.start()
@@ -459,7 +497,7 @@
         return jax.ShapeDtypeStruct(shape, dtype)
 
     square = scratch(1024, 1024)
-    wire = scratch(N, 16, 512)
+    wire = scratch(2 * N, 16, 256)
     x2, u2 = inputs.reshape(2, 512, 1024), cotangent.reshape(2, 512, 1024)
     kept = pl.pallas_call(
         mixer,
@@ -472,18 +510,19 @@
             scratch(2, 512, 512),
             scratch(2, 512, 512),
             scratch(4, 256, 256),
-            scratch(4, 256, 256),
             scratch(8, 16, 512),
             scratch(2, 512, 512),
             scratch(2, 512, 512),
         ),
         in_specs=[hbm, hbm, vmem, hbm, hbm],
-        out_specs=(vmem,) * 11,
+        out_specs=(vmem,) * 10,
         scratch_shapes=[scratch(2, 512, 512), scratch(4, 256, 256)]
         + [wire] * 7
         + [scratch(4, 4, 4, 2, 16, 512)]
-        + [square] * 9
-        + [scratch(1024, 256)]
+        + [square]
+        + [scratch(512, 512)] * 3
+        + [square] * 5
+        + [scratch(512, 256)]
         + [scratch(4, 4, 4, 16, 512)] * 3
         + [scratch(4, 16, 512)]
         + [pltpu.SemaphoreType.DMA((n,)) for n in (8, 8, 10, 8, 10, 18)],
@@ -503,7 +542,7 @@
             array(4, 256, 256, dtype=F32),
             array(8, 1024, dtype=F32),
         ),
-        in_specs=[vmem] * 11,
+        in_specs=[vmem] * 10,
         out_specs=(hbm,) * 5,
         scratch_shapes=[
             scratch(2, 512, 512),

time: 242 us -> 235 us (0.971)
  Pallas kernels: 241 us -> 234 us
    pallas_call x1, Pallas kernels: 238 us -> 231 us  [body(): pl.pallas_call(mixer, name='mixer', out_shape=(square, square, wire, scra...]
where the time goes in v5:
time: 235 us
  Pallas kernels  234 us (100%)
    pallas_call x1, Pallas kernels, body(): pl.pallas_call(mixer, name='mixer', out_shape=(square, square, wire, scra...  231 us

profile of v5, /device:TPU:1, one launch (start us, length us, event | category | flops | bytes accessed | tf_op | source)
XLA Modules:
  0.0 235.0 jit_solution(17085005193343793120)
XLA Ops:
  0.6 231.1 %mixer.1 = (bf16[1024,1024]{1,0:T(8,128)(2,1)S(1)}, bf16[1024,1024]{1,0:T(8,128)(2,1)S(1)}, bf16[256,16,256]{2,1,0:T(8,128)(2,1)S(1)}, f32[1024,1024]{1,0:T(8,12...) custom-call(bf16[2,512,1024]{2,1,0:T(8,128)(2,1)} %bitcast.4, ...), custom_call_target="tpu_custom_call" | custom-call | flops 25999998976 | bytes 14000000 | tf_op jit(solution)/shard_map/mixer/pallas_call | solution.py:502
  231.7 3.3 %finish.1 = (bf16[2,512,1024]{2,1,0:T(8,128)(2,1)}, bf16[2,512,1024]{2,1,0:T(8,128)(2,1)}, f32[2,512,512]{2,1,0:T(8,128)}, f32[4,256,256]{2,1,0:T(8,128)}, f32[8,1024]{1,0:T(8,128)}) custom-call(bf16[1024,1024]{1,0:T(8,128)(2,1)S(1)} %get-tuple-element.20.x_ref, bf16[1024,1024]{1,0:T(8,128)(2,1)S(1)} %get-tuple-element.21.u_ref, ...), custom_call_target="tpu_custom_call" | custom-call | flops 10000000 | bytes 7000000 | tf_op jit(solution)/shard_map/finish/pallas_call | solution.py:535

commit v6 on v5

--- a/solution.py
+++ b/solution.py
@@ -142,11 +142,15 @@
     def exchange(i, m, src, dst):
         own(i, m, src, dst).start()
 
+        give = to_source if i >= 2 else to_owner
+
         def send(k):
-            q, group = lax.rem(me + lax.div(k + 1, 2), N), lax.rem(dp + k + 1, 2)
-            (to_source if i >= 2 else to_owner)(i, m, src, dst, q, group)
-
-        loop(2 * N - 1, send)
+            q = lax.rem(me + k + 1, N)
+            give(i, m, src, dst, q, dp)
+            give(i, m, src, dst, q, 1 - dp)
+
+        loop(N - 1, send)
+        give(i, m, src, dst, me, 1 - dp)
 
     def arrived(i, m, src, dst):
         own(i, m, src, dst).wait()
@@ -167,18 +171,25 @@
                     src.at[a, pl.ds(b0, 32)], dst.at[pl.ds(512 * a + b0, 32)], in_sem.at[j]
                 ).start()
 
-    loop(16, load)
+    loop(4, load)
+
+    ready = pltpu.get_barrier_semaphore()
+
+    def greet(group, target):
+        pl.semaphore_signal(ready, inc=1, device_id=(group, target), device_id_type=MESH)
+
+    def greet_both(k):
+        q = lax.rem(me + k + 1, N)
+        greet(dp, q)
+        greet(1 - dp, q)
+
+    loop(N - 1, greet_both)
+    greet(1 - dp, me)
+    loop(12, lambda j: load(j + 4))
     left_in = pltpu.make_async_copy(l_hbm, l_ref, in_sem.at[16])
     left_in.start()
     right_in = pltpu.make_async_copy(r_hbm, r_ref, in_sem.at[17])
     right_in.start()
-
-    ready = pltpu.get_barrier_semaphore()
-
-    def greet(group, target):
-        pl.semaphore_signal(ready, inc=1, device_id=(group, target), device_id_type=MESH)
-
-    loop(2 * N - 1, lambda k: greet(lax.rem(dp + k + 1, 2), lax.rem(me + lax.div(k + 1, 2), N)))
 
     def second_grad(j):
         i = piece(j)
@@ -192,14 +203,15 @@
 
     def second_grad_out(j):
         def send(k):
-            d = 8 * piece(j) + lax.rem(me + lax.div(k, 2), 8)
-            group = lax.rem(dp + k, 2)
-
-            @pl.when((d != me) | (group != dp))
+            d = 8 * piece(j) + lax.rem(me + k, 8)
+
+            @pl.when(d != me)
             def _():
-                to_owner(0, 0, s1, r1, d, group)
-
-        loop(16, send)
+                to_owner(0, 0, s1, r1, d, dp)
+
+            to_owner(0, 0, s1, r1, d, 1 - dp)
+
+        loop(8, send)
 
     for m in range(2):
         rows = w_ref[:, 512 * m : 512 * m + 512].astype(F32).reshape(1, 8, 512)

time: 235 us -> 234 us (level)
  no operation moved by 1% of the time
where the time goes in v6:
time: 234 us
  Pallas kernels  233 us (100%)
    pallas_call x1, Pallas kernels, body(): pl.pallas_call(mixer, name='mixer', out_shape=(square, square, wire, scra...  230 us

profile of v6, /device:TPU:1, one launch (start us, length us, event | category | flops | bytes accessed | tf_op | source)
XLA Modules:
  0.0 233.5 jit_solution(5609069644404097935)
XLA Ops:
  0.6 229.6 %mixer.1 = (bf16[1024,1024]{1,0:T(8,128)(2,1)S(1)}, bf16[1024,1024]{1,0:T(8,128)(2,1)S(1)}, bf16[256,16,256]{2,1,0:T(8,128)(2,1)S(1)}, f32[1024,1024]{1,0:T(8,12...) custom-call(bf16[2,512,1024]{2,1,0:T(8,128)(2,1)} %bitcast.4, ...), custom_call_target="tpu_custom_call" | custom-call | flops 25999998976 | bytes 14000000 | tf_op jit(solution)/shard_map/mixer/pallas_call | solution.py:514
  230.2 3.3 %finish.1 = (bf16[2,512,1024]{2,1,0:T(8,128)(2,1)}, bf16[2,512,1024]{2,1,0:T(8,128)(2,1)}, f32[2,512,512]{2,1,0:T(8,128)}, f32[4,256,256]{2,1,0:T(8,128)}, f32[8,1024]{1,0:T(8,128)}) custom-call(bf16[1024,1024]{1,0:T(8,128)(2,1)S(1)} %get-tuple-element.20.x_ref, bf16[1024,1024]{1,0:T(8,128)(2,1)S(1)} %get-tuple-element.21.u_ref, ...), custom_call_target="tpu_custom_call" | custom-call | flops 10000000 | bytes 7000000 | tf_op jit(solution)/shard_map/finish/pallas_call | solution.py:547
